TPU v7x, 128 devices: a whole 4x4x4 slice. The times are simulated.
128 devices in a mesh: dev: 128 (over y, z, x, core).
Axes of the slice: x: 4, y: 4, z: 4, core: 2. Of those that a mesh axis runs over, the one named last changes fastest.
Arguments:
- spectrum: float32 [32768, 1296], P('dev'), may hold values from 0.01 to 2
- wind_speed: float32 [32768], P('dev'), may hold values from 0.2 to 2
- wind_dir: float32 [32768], P('dev'), may hold values from -3.140625 to 3.140625
- coupling: float32 [36, 36], replicated, may hold values from -1 to 1
- land_mask: int32 [96, 512], replicated, may hold values from 0 to 1, as said below
- sea_index: int32 [32768], replicated, may hold values from 0 to 49151, as said below
Outputs:
- updated: float32 [32768, 1296], P('dev')
Inputs may be any that keep to these rules, and one draw needn't show every extreme that they name: land_mask is 1 at exactly the 32768 cells named in sea_index; land comes in blocks of 8 x 8 cells of mixed shares. sea_index holds 32768 different cells, the first and the last cell of the grid among them. With the sea cells in increasing order as s_0, s_1, ..., row d * 256 + i holds s_(i * 128 + d).
All inputs are finite; a program needn't handle non-finite values.
Results may differ from a plain program's by a relative error of at most 0.0003.
Values sent between devices are 32-bit elements; how exact they have to be, the bound alone decides.
No kernel may reach another device: no remote copies, remote signals or barrier semaphores. Data moves between devices by JAX's collectives and lax.ppermute only.
A program may use at most 320 MiB of HBM per device.

v0:
```python
import jax
import jax.numpy as jnp
from jax import lax
from jax.sharding import PartitionSpec as P

NDIR = 36
NFREQ = 36
SUB = 4


def source_terms(spectrum, wind_speed, wind_dir, coupling):
    rows = spectrum.shape[0]
    angles = jnp.arange(NDIR).astype(jnp.float32) * (2.0 * jnp.pi / NDIR)
    phases = (jnp.arange(NFREQ).astype(jnp.float32) + 1.0) / NFREQ
    energy = jnp.mean(spectrum, axis=1)
    shaped = spectrum.reshape(rows, NDIR, NFREQ)
    align = jnp.maximum(jnp.cos(angles[None, :] - wind_dir[:, None]), 0.0)
    growth = wind_speed[:, None, None] * align[:, :, None] * phases[None, None, :]
    damping = 0.5 * jnp.sqrt(energy / (energy + 1.0))[:, None, None] * phases[None, None, :]
    relaxed = shaped * jnp.exp(growth - damping)
    transfer = jnp.einsum("pdf,fg->pdg", relaxed, coupling, precision=lax.Precision.HIGHEST)
    return (relaxed + 0.2 * transfer).reshape(rows, NDIR * NFREQ)


def advect(fields, xspeed, yspeed, seamask):
    for step in range(SUB):
        low_x = jnp.pad(fields[:, :-1, :], ((0, 0), (1, 0), (0, 0)))
        high_x = jnp.pad(fields[:, 1:, :], ((0, 0), (0, 1), (0, 0)))
        low_y = jnp.pad(fields[:, :, :-1], ((0, 0), (0, 0), (1, 0)))
        high_y = jnp.pad(fields[:, :, 1:], ((0, 0), (0, 0), (0, 1)))
        upwind_x = jnp.where(xspeed > 0, low_x, high_x)
        upwind_y = jnp.where(yspeed > 0, low_y, high_y)
        fields = seamask * (
            fields - jnp.abs(xspeed) * (fields - upwind_x) - jnp.abs(yspeed) * (fields - upwind_y)
        )
    return fields


def propagate(values, bin_ids, land_mask, sea_index, sample_index):
    bins = NDIR * NFREQ
    nxg, nyg = land_mask.shape
    seamask = land_mask.astype(jnp.float32)[None]
    dir_ids = (bin_ids // NFREQ).astype(jnp.float32)
    freq_ids = (bin_ids % NFREQ).astype(jnp.float32)
    speeds = jnp.where(bin_ids < bins, 0.45 * 1.1 ** (-freq_ids), 0.0)
    angle = dir_ids * (2.0 * jnp.pi / NDIR)
    xspeed = (speeds * jnp.cos(angle))[:, None, None]
    yspeed = (speeds * jnp.sin(angle))[:, None, None]
    count = values.shape[0]
    grid = jnp.zeros((count, nxg * nyg), jnp.float32).at[:, sea_index].set(values)
    moved = advect(grid.reshape(count, nxg, nyg), xspeed, yspeed, seamask)
    return moved.reshape(count, nxg * nyg)[:, sample_index]


def on_device(spectrum, wind_speed, wind_dir, coupling, land_mask, sea_index):
    forced = source_terms(spectrum, wind_speed, wind_dir, coupling)
    bins = NDIR * NFREQ
    ndev = lax.axis_size("dev")
    bin_slots = (bins + ndev - 1) // ndev
    outgoing = jnp.pad(forced, ((0, 0), (0, bin_slots * ndev - bins)))
    owned_bins = lax.axis_index("dev") * bin_slots + jnp.arange(bin_slots)
    owned = lax.all_to_all(outgoing.T, "dev", split_axis=0, concat_axis=1, tiled=True)
    sampled = propagate(owned, owned_bins, land_mask, sea_index, sea_index)
    back = lax.all_to_all(sampled, "dev", split_axis=1, concat_axis=0, tiled=True)
    return back[:bins].T


def solution(mesh):
    in_specs = (P("dev", None), P("dev"), P("dev"), P(), P(), P())
    out_specs = P("dev", None)
    return jax.shard_map(
        on_device, mesh=mesh, in_specs=in_specs, out_specs=out_specs, check_vma=False
    )
```

profile of v0, /device:TPU:1, one launch (start us, length us, event | category | flops | bytes accessed | tf_op | source)
XLA Modules:
  0.0 776.1 jit_solution(10433568125047300368)
XLA Ops:
  0.0 0.0 copy-start
  0.0 1.4 reshape.150
  1.4 1.5 reduce_sum.9
  3.0 0.9 maximum_multiply_fusion
  3.9 0.0 copy-done
  3.9 3.4 multiply_add_fusion
  7.3 1.4 reshape.151
  8.7 0.1 pad_bitcast_fusion
  8.8 1.5 all_to_all.28
  10.3 11.5 %all-to-all-start = ((f32[128,11,256]{2,1,0:T(8,128)}), f32[128,11,256]{2,1,0:T(8,128)S(1)}, u32[]{:S(2)}, u32[]{:S(2)}) async-start(f32[128,11,256]{2,1,0:T(8,128)} %all_to_all.28), calls=%async_computation | async-start | bytes 4194304 | tf_op jit(solution)/shard_map/all_to_all | solution.py:62
  21.9 0.9 convert_element_type.71
  22.8 0.1 fusion.13
  22.9 0.1 broadcast_compare_fusion
  22.9 1.6 broadcast_clamp_fusion
  24.5 27.9 %all-to-all-done = f32[128,11,256]{2,1,0:T(8,128)S(1)} async-done(((f32[128,11,256]{2,1,0:T(8,128)}), f32[128,11,256]{2,1,0:T(8,128)S(1)}, u32[]{:S(2)}, u32[]{:S(2)}) %all-to-all-start) | async-done | bytes 1441824 | tf_op jit(solution)/shard_map/all_to_all | solution.py:62
  52.4 0.8 copy.13
  53.2 0.2 pad.74
  53.4 1.2 copy.18
  54.7 8.8 %copy.14 = f32[32768,11]{1,0:T(8,128)} copy(f32[32768,11]{0,1:T(8,128)S(1)} %bitcast.29) | data formatting | bytes 2883584 | tf_op jit(solution)/shard_map/all_to_all | solution.py:62
  63.5 90.3 %scatter_custom_fusion = f32[11,49152]{0,1:T(8,128)} fusion(s32[32768]{0:T(1024)S(1)} %get-tuple-element.22, f32[32768,11]{1,0:T(8,128)} %copy.14, f32[]{:T(128)} %constant.17.clone.1), kind=kCustom, calls=%fused_computation.6 | custom fusion | bytes 2163200 | tf_op jit(solution)/shard_map/scatter | solution.py:50
  153.8 31.8 %fusion.21 = (f32[11,95,512]{0,2,1:T(8,128)}, f32[11,95,512]{0,2,1:T(8,128)}) fusion(f32[11,96,512]{0,2,1:T(8,128)} %bitcast.24), kind=kLoop, calls=%fused_computation.47 | loop fusion | bytes 8560640 | tf_op jit(solution)/shard_map/slice | solution.py:27
  185.6 33.6 %fusion.22 = (f32[11,96,511]{0,2,1:T(8,128)}, f32[11,96,511]{0,2,1:T(8,128)}) fusion(f32[11,96,512]{0,2,1:T(8,128)} %bitcast.25), kind=kLoop, calls=%fused_computation.48 | loop fusion | bytes 8633856 | tf_op jit(solution)/shard_map/slice | solution.py:29
  219.2 48.9 %subtract_multiply_fusion.3 = f32[11,96,512]{0,2,1:T(8,128)} fusion(f32[11,96,512]{0,2,1:T(8,128)} %bitcast.26, f32[11,96,511]{0,2,1:T(8,128)} %get-tuple-element.20, f32[11,96,511]{0,2,1:T(8,128)} %get-tuple-element.19, f32[11,95,512]{0,2,1:T(8,128)} %get-tuple-element.18, f32[11,95,512]{0,2,1:T(8,128)} %get-tuple-element.17, f32[11]{0:T(128)S(1)} %get-tuple-element.28, ...), kind=kLoop, calls=%fused_computation.5 | loop fusion | flops 4866048 | bytes 13119342 | tf_op jit(solution)/shard_map/mul | solution.py:33
  268.1 31.8 %fusion.19 = (f32[11,95,512]{0,2,1:T(8,128)}, f32[11,95,512]{0,2,1:T(8,128)}) fusion(f32[11,96,512]{0,2,1:T(8,128)} %subtract_multiply_fusion.3), kind=kLoop, calls=%fused_computation.45 | loop fusion | bytes 8560640 | tf_op jit(solution)/shard_map/slice | solution.py:27
  299.9 33.6 %fusion.20 = (f32[11,96,511]{0,2,1:T(8,128)}, f32[11,96,511]{0,2,1:T(8,128)}) fusion(f32[11,96,512]{0,2,1:T(8,128)} %subtract_multiply_fusion.3), kind=kLoop, calls=%fused_computation.46 | loop fusion | bytes 8633856 | tf_op jit(solution)/shard_map/slice | solution.py:29
  333.5 48.9 %subtract_multiply_fusion.2 = f32[11,96,512]{0,2,1:T(8,128)} fusion(f32[11,96,512]{0,2,1:T(8,128)} %subtract_multiply_fusion.3, f32[11,96,511]{0,2,1:T(8,128)} %get-tuple-element.16, f32[11,96,511]{0,2,1:T(8,128)} %get-tuple-element.15, f32[11,95,512]{0,2,1:T(8,128)} %get-tuple-element.14, f32[11,95,512]{0,2,1:T(8,128)} %get-tuple-element.13, ...), kind=kLoop, calls=%fused_computation.4 | loop fusion | flops 4866048 | bytes 13119342 | tf_op jit(solution)/shard_map/mul | solution.py:33
  382.4 31.8 %fusion.17 = (f32[11,95,512]{0,2,1:T(8,128)}, f32[11,95,512]{0,2,1:T(8,128)}) fusion(f32[11,96,512]{0,2,1:T(8,128)} %subtract_multiply_fusion.2), kind=kLoop, calls=%fused_computation.43 | loop fusion | bytes 8560640 | tf_op jit(solution)/shard_map/slice | solution.py:27
  414.2 33.6 %fusion.18 = (f32[11,96,511]{0,2,1:T(8,128)}, f32[11,96,511]{0,2,1:T(8,128)}) fusion(f32[11,96,512]{0,2,1:T(8,128)} %subtract_multiply_fusion.2), kind=kLoop, calls=%fused_computation.44 | loop fusion | bytes 8633856 | tf_op jit(solution)/shard_map/slice | solution.py:29
  447.8 48.9 %subtract_multiply_fusion.1 = f32[11,96,512]{0,2,1:T(8,128)} fusion(f32[11,96,512]{0,2,1:T(8,128)} %subtract_multiply_fusion.2, f32[11,96,511]{0,2,1:T(8,128)} %get-tuple-element.12, f32[11,96,511]{0,2,1:T(8,128)} %get-tuple-element.11, f32[11,95,512]{0,2,1:T(8,128)} %get-tuple-element.10, f32[11,95,512]{0,2,1:T(8,128)} %get-tuple-element.9, ...), kind=kLoop, calls=%fused_computation.3 | loop fusion | flops 4866048 | bytes 13119342 | tf_op jit(solution)/shard_map/mul | solution.py:33
  496.7 31.8 %fusion.15 = (f32[11,95,512]{0,2,1:T(8,128)}, f32[11,95,512]{0,2,1:T(8,128)}) fusion(f32[11,96,512]{0,2,1:T(8,128)} %subtract_multiply_fusion.1), kind=kLoop, calls=%fused_computation.41 | loop fusion | bytes 8560640 | tf_op jit(solution)/shard_map/slice | solution.py:27
  528.6 33.8 %fusion.16 = (f32[11,96,511]{0,2,1:T(8,128)}, f32[11,96,511]{0,2,1:T(8,128)}) fusion(f32[11,96,512]{0,2,1:T(8,128)} %subtract_multiply_fusion.1), kind=kLoop, calls=%fused_computation.42 | loop fusion | bytes 8633856 | tf_op jit(solution)/shard_map/slice | solution.py:29
  562.4 0.0 copy-start.2
  562.4 0.0 copy-start.1
  562.4 48.9 %subtract_multiply_fusion = f32[11,96,512]{0,2,1:T(8,128)} fusion(f32[11,96,512]{0,2,1:T(8,128)} %subtract_multiply_fusion.1, f32[11,96,511]{0,2,1:T(8,128)} %get-tuple-element.8, f32[11,96,511]{0,2,1:T(8,128)} %get-tuple-element.7, f32[11,95,512]{0,2,1:T(8,128)} %get-tuple-element.6, f32[11,95,512]{0,2,1:T(8,128)} %get-tuple-element.5, ...), kind=kLoop, calls=%fused_computation.2 | loop fusion | flops 4866048 | bytes 13119342 | tf_op jit(solution)/shard_map/mul | solution.py:33
  611.3 0.0 copy-done.2
  611.3 117.0 %gather_fusion = f32[32768,11]{1,0:T(8,128)} fusion(f32[11,49152]{0,1:T(8,128)} %bitcast.27, s32[32768]{0:T(1024)S(1)} %copy-done.2), kind=kCustom, calls=%fused_computation | custom fusion | bytes 3014656 | tf_op jit(solution)/shard_map/gather | solution.py:52
  728.3 10.0 %copy.15 = f32[11,128,256]{2,0,1:T(8,128)S(1)} copy(f32[11,128,256]{0,2,1:T(8,128)} %bitcast.28) | data formatting | bytes 2883584 | tf_op jit(solution)/shard_map/all_to_all | solution.py:64
  738.3 35.1 %all_to_all.38 = f32[11,128,256]{2,0,1:T(8,128)} all-to-all(f32[11,128,256]{2,0,1:T(8,128)S(1)} %copy.15), channel_id=1, replica_groups=mesh['dev'=128] {'dev'}, dimensions={1} | all-to-all | bytes 2883584 | tf_op jit(solution)/shard_map/all_to_all | solution.py:64
  773.4 1.6 all_to_all.35
  775.0 1.1 slice_bitcast_fusion
  776.1 0.0 copy-done.1
  (3 shorter events, 0.0 us)
Async XLA Ops:
  0.0 3.9 copy-start
  10.3 42.0 %all-to-all-start = ((f32[128,11,256]{2,1,0:T(8,128)}), f32[128,11,256]{2,1,0:T(8,128)S(1)}, u32[]{:S(2)}, u32[]{:S(2)}) async-start(f32[128,11,256]{2,1,0:T(8,128)} %all_to_all.28), calls=%async_computation | async-start | bytes 4194304 | tf_op jit(solution)/shard_map/all_to_all | solution.py:62
  562.4 48.9 %copy-start.2 = (s32[32768]{0:T(1024)S(1)}, s32[32768]{0:T(1024)}, u32[]{:S(2)}) copy-start(s32[32768]{0:T(1024)} %get-tuple-element.21) | copy-start | bytes 393220
  562.4 213.8 %copy-start.1 = (f32[36,36]{1,0:T(8,128)S(1)}, f32[36,36]{1,0:T(8,128)}, u32[]{:S(2)}) copy-start(f32[36,36]{1,0:T(8,128)} %param.9) | copy-start | bytes 15556
where the time goes:
time: 777 us; the launch traced here: 776 us
  local copies, waits for them, and re-layouts  498 us (64%)
  other arithmetic  201 us (26%)
  blocking collectives  35.1 us (5%)
  waiting for transfers between devices  27.9 us (4%)
  starting transfers between devices  11.5 us (1%)
    mul x4, other arithmetic, advect(): seamask * (fields - jnp.abs(xspeed) * (fields - upwind_x) - jnp.abs(yspee...  196 us
    slice x4, local copies, waits for them, and re-layouts, advect(): low_y = jnp.pad(fields[:, :, :-1], ((0, 0), (0, 0), (1, 0)))  135 us
    slice x4, local copies, waits for them, and re-layouts, advect(): low_x = jnp.pad(fields[:, :-1, :], ((0, 0), (1, 0), (0, 0)))  127 us
    gather x1, local copies, waits for them, and re-layouts, propagate(): return moved.reshape(count, nxg * nyg)[:, sample_index]  117 us
    scatter x1, local copies, waits for them, and re-layouts, propagate(): jnp.zeros((count, nxg * nyg), jnp.float32).at[:, sea_index].set(values)  90.3 us
    all_to_all x1, blocking collectives, on_device(): lax.all_to_all(sampled, 'dev', split_axis=1, concat_axis=0, tiled=True)  35.1 us
    all_to_all x1, waiting for transfers between devices, on_device(): lax.all_to_all(outgoing.T, 'dev', split_axis=0, concat_axis=1, tiled=True)  27.9 us
  transfers between devices with their start and end apart: 1, of which 1 were waited for; matrix products, arithmetic and copies ran while one was open for 0% of the time, Pallas kernels for 0%

commit v1 on v0

v1 whole, which is shorter than its diff:
```python
import jax
import jax.numpy as jnp
from jax import lax
from jax.experimental import pallas as pl
from jax.experimental.pallas import tpu as pltpu
from jax.sharding import PartitionSpec as P

NDIR = 36
NFREQ = 36
BINS = NDIR * NFREQ
SUB = 4
NXG = 96
NYG = 512
N_DEV = 128
P_DEV = 256
LANES = 128
COLS = NYG // LANES
BLOCKS = NXG * COLS
QUAD = BINS // 4
QDEV = N_DEV // 4
SLOTS = -(-QUAD // QDEV)
QPAD = SLOTS * QDEV
GROUP = 16
HALVES = P_DEV // LANES
CHUNK = SLOTS * HALVES
ROWS = N_DEV * CHUNK
PAIR = 2 * NFREQ
VMEM = 48 * 1024 * 1024


def source_kernel(spec_ref, speed_ref, dir_ref, coupling_ref, out_ref, amp_ref):
    f32 = jnp.float32
    energy = jnp.sum(spec_ref[...], axis=0, keepdims=True) * (1.0 / BINS)
    damp = 0.5 * jnp.sqrt(energy / (energy + 1.0))
    angles = lax.broadcasted_iota(jnp.int32, (40, P_DEV), 0).astype(f32) * (2.0 * jnp.pi / NDIR)
    align = jnp.maximum(jnp.cos(angles - dir_ref[...]), 0.0)
    amp_ref[...] = speed_ref[...] * align - damp

    row = lax.broadcasted_iota(jnp.int32, (PAIR, NFREQ), 0)
    col = lax.broadcasted_iota(jnp.int32, (PAIR, NFREQ), 1)
    spread = jnp.where(jnp.where(row >= NFREQ, row - NFREQ, row) == col, 1.0, 0.0).astype(f32)
    dims = (((1,), (1,)), ((), ()))
    best = lax.Precision.HIGHEST
    tall = lax.dot_general(spread, coupling_ref[...], dims, precision=best, preferred_element_type=f32)
    both = lax.dot_general(tall, spread, dims, precision=best, preferred_element_type=f32)
    at = lax.broadcasted_iota(jnp.int32, (PAIR, PAIR), 0) >= NFREQ
    to = lax.broadcasted_iota(jnp.int32, (PAIR, PAIR), 1) >= NFREQ
    matrix = jnp.where(at == to, 0.2 * both, 0.0)

    place = lax.broadcasted_iota(jnp.int32, (PAIR, P_DEV), 0)
    first = place < NFREQ
    phase = (jnp.where(first, place, place - NFREQ).astype(f32) + 1.0) * (1.0 / NFREQ)

    for quad in range(4):
        begin = 2 * (QPAD * quad + 320)
        out_ref[begin : begin + 64, :] = jnp.zeros((64, LANES), f32)

    for pair in range(NDIR // 2):
        low = amp_ref[2 * pair : 2 * pair + 1, :]
        high = amp_ref[2 * pair + 1 : 2 * pair + 2, :]
        relaxed = spec_ref[PAIR * pair : PAIR * pair + PAIR, :] * jnp.exp(phase * jnp.where(first, low, high))
        forced = relaxed + lax.dot_general(
            matrix, relaxed, (((1,), (0,)), ((), ())), precision=best, preferred_element_type=f32
        )
        quad_low, quad_high = (2 * pair) // 9, (2 * pair + 1) // 9
        base = PAIR * pair + (QPAD - QUAD) * quad_low
        for half in range(HALVES):
            part = forced[:, half * LANES : (half + 1) * LANES]
            if quad_low == quad_high:
                out_ref[pl.ds(2 * base + half, PAIR, stride=2), :] = part
            else:
                other = PAIR * pair + (QPAD - QUAD) * quad_high + 32
                out_ref[pl.ds(2 * base + half, 40, stride=2), :] = part[:40]
                out_ref[pl.ds(2 * other + half, 40, stride=2), :] = part[32:]


def source_terms(spectrum, wind_speed, wind_dir, coupling):
    return pl.pallas_call(
        source_kernel,
        out_shape=jax.ShapeDtypeStruct((ROWS, LANES), jnp.float32),
        in_specs=[pl.BlockSpec(memory_space=pltpu.VMEM)] * 4,
        out_specs=pl.BlockSpec(memory_space=pltpu.VMEM),
        scratch_shapes=[pltpu.VMEM((40, P_DEV), jnp.float32)],
        compiler_params=pltpu.CompilerParams(vmem_limit_bytes=VMEM),
        name="source_terms",
    )(spectrum.T, wind_speed.reshape(1, P_DEV), wind_dir.reshape(1, P_DEV), coupling)


def propagate_kernel(meta_ref, recv_ref, index_ref, mask_ref, spot_ref, coef_ref, out_ref, src, dst, *bufs):
    f32 = jnp.float32
    bufs = [bufs[2 * s : 2 * s + 2] for s in range(SUB + 1)]
    up_x = meta_ref[BLOCKS + 1]
    up_y = meta_ref[BLOCKS + 2]
    lane = lax.broadcasted_iota(jnp.int32, (GROUP, LANES), 1)
    edge = lane == jnp.where(up_y > 0, 0, LANES - 1)
    shift = jnp.where(up_y > 0, 1, LANES - 1)

    for slot in range(SLOTS):
        for half in range(HALVES):
            part = recv_ref[pl.ds(HALVES * slot + half, N_DEV, stride=CHUNK), :]
            src[pl.ds(half * LANES * GROUP + slot, LANES, stride=GROUP), :] = part.T

    for pair in bufs:
        for buf in pair:
            buf[...] = jnp.zeros_like(buf)

    coef_stay = coef_ref[0:GROUP, :]
    coef_x = coef_ref[GROUP : 2 * GROUP, :]
    coef_y = coef_ref[2 * GROUP : 3 * GROUP, :]

    def block(row, j):
        row = jnp.clip(row, 0, NXG - 1)
        g = jnp.where(up_x > 0, row, NXG - 1 - row)
        return g * COLS + jnp.where(up_y > 0, j, COLS - 1 - j)

    def at(j):
        return slice(j * GROUP, (j + 1) * GROUP)

    def advance(t, p):
        for j in range(COLS):
            cell = block(t - SUB - 1, j)
            start = meta_ref[cell]
            count = meta_ref[cell + 1] - start
            line = start >> 7
            off = start & (LANES - 1)
            one = jnp.broadcast_to(spot_ref[pl.ds(line, 1), :], (GROUP, LANES))
            two = jnp.broadcast_to(spot_ref[pl.ds(line + 1, 1), :], (GROUP, LANES))
            spots = jnp.where(lane >= off, one, two)
            taken = jnp.take_along_axis(bufs[SUB][1 - p][at(j), :], spots, axis=1, mode="promise_in_bounds")
            end = jnp.where(t - SUB - 1 < NXG, off + count, 0)
            here = pl.ds(pl.multiple_of(line * GROUP, GROUP), GROUP)
            after = pl.ds(pl.multiple_of((line + 1) * GROUP, GROUP), GROUP)
            pltpu.store(dst.at[here, :], taken, mask=(lane >= off) & (lane < end))
            pltpu.store(dst.at[after, :], taken, mask=lane < end - LANES)

        for step in range(SUB, 0, -1):
            fields = [bufs[step - 1][1 - p][at(j), :] for j in range(COLS)]
            turned = [pltpu.roll(field, shift, 1) for field in fields]
            for j in range(COLS):
                upwind_x = bufs[step - 1][p][at(j), :]
                upwind_y = jnp.where(edge, turned[j - 1] if j else 0.0, turned[j])
                sea = mask_ref[pl.ds(block(t - step, j), 1), :]
                moved = coef_stay * fields[j] + coef_x * upwind_x + coef_y * upwind_y
                bufs[step][p][at(j), :] = sea * moved

        for j in range(COLS):
            cell = block(t, j)
            start = meta_ref[cell]
            line = start >> 7
            off = start & (LANES - 1)
            one = src[pl.ds(pl.multiple_of(line * GROUP, GROUP), GROUP), :]
            two = src[pl.ds(pl.multiple_of((line + 1) * GROUP, GROUP), GROUP), :]
            index = jnp.broadcast_to(index_ref[pl.ds(cell, 1), :], (GROUP, LANES))
            placed = jnp.take_along_axis(jnp.where(lane >= off, one, two), index, axis=1, mode="promise_in_bounds")
            bufs[0][p][at(j), :] = jnp.where(mask_ref[pl.ds(cell, 1), :] > 0, placed, 0.0)

    def two_rows(u, carry):
        advance(2 * u, 0)
        advance(2 * u + 1, 1)
        return carry

    lax.fori_loop(0, (NXG + SUB + 2) // 2, two_rows, 0)

    for slot in range(SLOTS):
        for half in range(HALVES):
            part = dst[pl.ds(half * LANES * GROUP + slot, LANES, stride=GROUP), :]
            out_ref[pl.ds(HALVES * slot + half, N_DEV, stride=CHUNK), :] = part.T


def propagate(recv, land_mask, sea_index):
    f32 = jnp.float32
    dev = lax.axis_index("dev")
    quad = dev // QDEV
    within = (dev % QDEV) * SLOTS + jnp.arange(GROUP)
    bins = quad * QUAD + within
    real = (within < QUAD) & (jnp.arange(GROUP) < SLOTS)
    speeds = jnp.where(real, 0.45 * 1.1 ** (-(bins % NFREQ).astype(f32)), 0.0)
    angle = (bins // NFREQ).astype(f32) * (2.0 * jnp.pi / NDIR)
    abs_x = jnp.abs(speeds * jnp.cos(angle))
    abs_y = jnp.abs(speeds * jnp.sin(angle))
    coef = jnp.broadcast_to(jnp.concatenate([1.0 - abs_x - abs_y, abs_x, abs_y])[:, None], (3 * GROUP, LANES))
    up_x = ((quad == 0) | (quad == 3)).astype(jnp.int32)
    up_y = (quad < 2).astype(jnp.int32)

    mask = land_mask.reshape(BLOCKS, LANES).astype(f32)
    upto = jnp.dot(mask, jnp.triu(jnp.ones((LANES, LANES), f32)), preferred_element_type=f32)
    before = jnp.dot(jnp.tril(jnp.ones((BLOCKS, BLOCKS), f32), -1), upto[:, LANES - 1 :], preferred_element_type=f32)
    index = (before + upto - mask).astype(jnp.int32) & (LANES - 1)
    starts = before[:, 0].astype(jnp.int32)
    meta = jnp.concatenate([starts, jnp.array([N_DEV * P_DEV], jnp.int32), up_x[None], up_y[None]])
    spot = jnp.pad((sea_index & (LANES - 1)).reshape(N_DEV, P_DEV).T, ((0, 8), (0, 0)))

    return pl.pallas_call(
        propagate_kernel,
        out_shape=jax.ShapeDtypeStruct((ROWS, LANES), f32),
        in_specs=[pl.BlockSpec(memory_space=pltpu.SMEM)] + [pl.BlockSpec(memory_space=pltpu.VMEM)] * 5,
        out_specs=pl.BlockSpec(memory_space=pltpu.VMEM),
        scratch_shapes=[pltpu.VMEM(((P_DEV + 2) * GROUP, LANES), f32)] * 2
        + [pltpu.VMEM((COLS * GROUP, LANES), f32)] * (2 * (SUB + 1)),
        compiler_params=pltpu.CompilerParams(vmem_limit_bytes=VMEM),
        name="propagate",
    )(meta, recv, index, mask, spot, coef)


def collect_kernel(in_ref, out_ref):
    for quad in (1, 0, 3, 2):
        lead = 4 * (quad % 2)
        for half in range(HALVES):
            part = in_ref[pl.ds(2 * (QPAD * quad - lead) + half, QUAD + lead, stride=2), :]
            out_ref[QUAD * quad - lead : QUAD * (quad + 1), half * LANES : (half + 1) * LANES] = part


def collect(back):
    return pl.pallas_call(
        collect_kernel,
        out_shape=jax.ShapeDtypeStruct((BINS, P_DEV), jnp.float32),
        in_specs=[pl.BlockSpec(memory_space=pltpu.VMEM)],
        out_specs=pl.BlockSpec(memory_space=pltpu.VMEM),
        compiler_params=pltpu.CompilerParams(vmem_limit_bytes=VMEM),
        name="collect",
    )(back)


def exchange(rows):
    swapped = lax.all_to_all(rows.reshape(ROWS, 1, LANES), "dev", split_axis=0, concat_axis=0, tiled=True)
    return swapped.reshape(ROWS, LANES)


def on_device(spectrum, wind_speed, wind_dir, coupling, land_mask, sea_index):
    sent = source_terms(spectrum, wind_speed, wind_dir, coupling)
    moved = propagate(exchange(sent), land_mask, sea_index)
    return collect(exchange(moved)).T


def solution(mesh):
    in_specs = (P("dev", None), P("dev"), P("dev"), P(), P(), P())
    return jax.shard_map(on_device, mesh=mesh, in_specs=in_specs, out_specs=P("dev", None), check_vma=False)
```

time: 777 us -> 84.2 us (0.11)
  local copies, waits for them, and re-layouts: 498 us -> 3.88 us
  other arithmetic: 201 us -> 0.38 us
  Pallas kernels: 0 us -> 17.8 us
    slice x8 -> x1, local copies, waits for them, and re-layouts: 262 us -> 0.23 us  [propagate(): upto[:, LANES - 1:]]
    mul x7 -> x0, other arithmetic: 197 us -> none  [the longest x4 196 us: advect(): seamask * (fields - jnp.abs(xspeed) * (fields - upwind_x) - jnp.abs(yspee...]
    gather x1 -> x0, local copies, waits for them, and re-layouts: 117 us -> none  [propagate(): return moved.reshape(count, nxg * nyg)[:, sample_index]]
    scatter x1 -> x0, local copies, waits for them, and re-layouts: 90.3 us -> none  [propagate(): jnp.zeros((count, nxg * nyg), jnp.float32).at[:, sea_index].set(values)]
    all_to_all x5 -> x0, local copies, waits for them, and re-layouts: 22.8 us -> none  [the longest x2 11.6 us: on_device(): lax.all_to_all(sampled, 'dev', split_axis=1, concat_axis=0, tiled=True)]
    pallas_call x0 -> x3, Pallas kernels: none -> 17.8 us  [the longest x1 13.8 us: propagate(): pl.pallas_call(propagate_kernel, out_shape=jax.ShapeDtypeStruct((ROWS, LA...]
  transfers between devices with their start and end apart: 1 -> 1, of which waited for: 1 -> 1; matrix products, arithmetic and copies ran while one was open for 0% -> 2% of each run, Pallas kernels for 0% -> 0%
where the time goes in v1:
time: 84.2 us; the launch traced here: 83.9 us
  blocking collectives  27.6 us (33%)
  waiting for transfers between devices  22.1 us (26%)
  Pallas kernels  17.8 us (21%)
  starting transfers between devices  11.5 us (14%)
  local copies, waits for them, and re-layouts  3.88 us (5%)
    all_to_all x1, blocking collectives, exchange(): lax.all_to_all(rows.reshape(ROWS, 1, LANES), 'dev', split_axis=0, concat_...  27.6 us
    all_to_all x1, waiting for transfers between devices, exchange(): lax.all_to_all(rows.reshape(ROWS, 1, LANES), 'dev', split_axis=0, concat_...  22.1 us
    pallas_call x1, Pallas kernels, propagate(): pl.pallas_call(propagate_kernel, out_shape=jax.ShapeDtypeStruct((ROWS, LA...  13.8 us
    all_to_all x1, starting transfers between devices, exchange(): lax.all_to_all(rows.reshape(ROWS, 1, LANES), 'dev', split_axis=0, concat_...  11.5 us
    unnamed x12, local copies, waits for them, and re-layouts  3.42 us
    pallas_call x1, Pallas kernels, source_terms(): pl.pallas_call(source_kernel, out_shape=jax.ShapeDtypeStruct((ROWS, LANES...  2.9 us
  transfers between devices with their start and end apart: 1, of which 1 were waited for; matrix products, arithmetic and copies ran while one was open for 2% of the time, Pallas kernels for 0%

profile of v1, /device:TPU:1, one launch (start us, length us, event | category | flops | bytes accessed | tf_op | source)
XLA Modules:
  0.0 83.9 jit_solution(16900147813229814236)
XLA Ops:
  0.0 0.0 copy-start
  0.0 1.3 %copy-done = f32[256,1296]{0,1:T(8,128)S(1)} copy-done((f32[256,1296]{0,1:T(8,128)S(1)}, f32[256,1296]{0,1:T(8,128)}, u32[]{:S(2)}) %copy-start) | copy-done | bytes 1327128
  1.3 0.0 copy-start.1
  1.3 0.7 copy-done.1
  2.1 0.0 copy-start.2
  2.1 0.7 copy-done.2
  2.7 0.0 copy-start.3
  2.7 0.7 copy-done.3
  3.4 2.9 %source_terms.1 = f32[2816,128]{1,0:T(8,128)} custom-call(f32[1296,256]{1,0:T(8,128)S(1)} %bitcast.22, f32[1,256]{1,0:T(1,128)S(1)} %bitcast.23, f32[1,256]{1,0:T(1,128)S(1)} %bitcast.24, f32[36,36]{1,0:T(8,128)S(1)} %copy-done.1), custom_call_target="tpu_custom_call" | custom-call | tf_op jit(solution)/shard_map/source_terms/pallas_call | solution.py:78
  6.3 0.0 copy-start.4
  6.3 11.5 %all-to-all-start = ((f32[2816,1,128]{2,1,0:T(1,128)}), f32[2816,1,128]{2,1,0:T(1,128)S(1)}, u32[]{:S(2)}, u32[]{:S(2)}) async-start(f32[2816,1,128]{2,1,0:T(1,128)} %bitcast.7), calls=%async_computation | async-start | bytes 2883584 | tf_op jit(solution)/shard_map/all_to_all | solution.py:225
  17.8 0.0 copy-start.5
  17.9 0.0 copy-done.4
  17.9 0.2 convolution_bitcast_fusion
  18.2 0.2 slice_reduce_fusion
  18.4 0.3 convolution_reduce_fusion
  18.7 0.0 copy-done.5
  18.8 0.1 copy.13
  18.9 0.1 subtract_subtract_fusion
  19.0 0.1 pad_maximum_fusion
  19.1 0.1 pad_add_fusion.meta_ref
  19.2 0.1 convert_and_fusion.index_ref
  19.3 22.1 %all-to-all-done = f32[2816,1,128]{2,1,0:T(1,128)S(1)} async-done(((f32[2816,1,128]{2,1,0:T(1,128)}), f32[2816,1,128]{2,1,0:T(1,128)S(1)}, u32[]{:S(2)}, u32[]{:S(2)}) %all-to-all-start) | async-done | bytes 1441824 | tf_op jit(solution)/shard_map/all_to_all | solution.py:225
  41.3 0.1 broadcast_in_dim.45.coef_ref
  41.4 13.8 %propagate.1 = f32[2816,128]{1,0:T(8,128)S(1)} custom-call(s32[387]{0:T(512)S(1)} %pad_add_fusion.meta_ref, f32[2816,128]{1,0:T(8,128)S(1)} %bitcast.19, s32[384,128]{1,0:T(8,128)S(1)} %convert_and_fusion.index_ref, f32[384,128]{1,0:T(8,128)S(1)} %convert_element_type.20.mask_ref, s32[264,128]{1,0:T(8,128)S(1)} %pad.4.spot_ref, ...), custom_call_target="tpu_custom_call" | custom-call | tf_op jit(solution)/shard_map/propagate/pallas_call | solution.py:193
  55.2 27.6 %all_to_all.10 = f32[2816,1,128]{2,1,0:T(1,128)S(1)} all-to-all(f32[2816,1,128]{2,1,0:T(1,128)S(1)} %bitcast.20), channel_id=1, replica_groups=mesh['dev'=128] {'dev'}, dimensions={0} | all-to-all | bytes 2883584 | tf_op jit(solution)/shard_map/all_to_all | solution.py:225
  82.8 1.1 %collect.1 = f32[1296,256]{1,0:T(8,128)} custom-call(f32[2816,128]{1,0:T(8,128)S(1)} %bitcast.21), custom_call_target="tpu_custom_call" | custom-call | tf_op jit(solution)/shard_map/collect/pallas_call | solution.py:214
  (9 shorter events, 0.1 us)
Async XLA Ops:
  0.0 1.3 %copy-start = (f32[256,1296]{0,1:T(8,128)S(1)}, f32[256,1296]{0,1:T(8,128)}, u32[]{:S(2)}) copy-start(f32[256,1296]{0,1:T(8,128)} %param.7) | copy-start | bytes 3981316
  1.3 0.7 copy-start.1
  2.1 0.7 copy-start.2
  2.7 0.7 copy-start.3
  6.3 11.6 %copy-start.4 = (s32[96,512]{1,0:T(8,128)S(1)}, s32[96,512]{1,0:T(8,128)}, u32[]{:S(2)}) copy-start(s32[96,512]{1,0:T(8,128)} %param.11) | copy-start | bytes 589828
  6.3 35.0 %all-to-all-start = ((f32[2816,1,128]{2,1,0:T(1,128)}), f32[2816,1,128]{2,1,0:T(1,128)S(1)}, u32[]{:S(2)}, u32[]{:S(2)}) async-start(f32[2816,1,128]{2,1,0:T(1,128)} %bitcast.7), calls=%async_computation | async-start | bytes 2883584 | tf_op jit(solution)/shard_map/all_to_all | solution.py:225
  17.8 0.9 %copy-start.5 = (s32[32768]{0:T(1024)S(1)}, s32[32768]{0:T(1024)}, u32[]{:S(2)}) copy-start(s32[32768]{0:T(1024)} %param.12) | copy-start | bytes 393220

commit v2 on v1

v2 whole, which is shorter than its diff:
```python
import jax
import jax.numpy as jnp
from jax import lax
from jax.experimental import pallas as pl
from jax.experimental.pallas import tpu as pltpu
from jax.sharding import PartitionSpec as P

NDIR = 36
NFREQ = 36
BINS = NDIR * NFREQ
SUB = 4
NXG = 96
NYG = 512
N_DEV = 128
P_DEV = 256
LANES = 128
COLS = NYG // LANES
BLOCKS = NXG * COLS
QUAD = BINS // 4
QDEV = N_DEV // 4
SLOTS = -(-QUAD // QDEV)
QPAD = SLOTS * QDEV
GROUP = 16
HALVES = P_DEV // LANES
CHUNK = SLOTS * HALVES
ROWS = N_DEV * CHUNK
PAIR = 2 * NFREQ
PARTS = 6
PART = BINS // PARTS
SLAB = 2
SLABS = NXG // SLAB
STEP = SLAB * COLS
MERGE_OUT = False
DELAY = SUB if MERGE_OUT else SUB + 1
ROUNDS = -(-(SLABS + DELAY) // 2) * 2
ALONG_LANES = lax.GatherDimensionNumbers(
    offset_dims=(),
    collapsed_slice_dims=(1,),
    start_index_map=(1,),
    operand_batching_dims=(0,),
    start_indices_batching_dims=(0,),
)
VMEM = 48 * 1024 * 1024


def source_kernel(spec_hbm, speed_hbm, dir_hbm, coupling_hbm, out_hbm, spec, speed, dirs, coupling, amp, out, in_sems, out_sems):
    f32 = jnp.float32
    small = [
        pltpu.make_async_copy(source, target, in_sems.at[PARTS + at])
        for at, (source, target) in enumerate(((speed_hbm, speed), (dir_hbm, dirs), (coupling_hbm, coupling)))
    ]
    loads = [
        pltpu.make_async_copy(spec_hbm.at[part, :], spec.at[part, :], in_sems.at[at])
        for at, part in enumerate(pl.ds(at * PART, PART) for at in range(PARTS))
    ]
    for copy in small + loads:
        copy.start()
    for copy in small:
        copy.wait()

    row = lax.broadcasted_iota(jnp.int32, (PAIR, NFREQ), 0)
    col = lax.broadcasted_iota(jnp.int32, (PAIR, NFREQ), 1)
    spread = jnp.where(jnp.where(row >= NFREQ, row - NFREQ, row) == col, 1.0, 0.0).astype(f32)
    dims = (((1,), (1,)), ((), ()))
    best = lax.Precision.HIGHEST
    tall = lax.dot_general(spread, coupling[...], dims, precision=best, preferred_element_type=f32)
    both = lax.dot_general(tall, spread, dims, precision=best, preferred_element_type=f32)
    at = lax.broadcasted_iota(jnp.int32, (PAIR, PAIR), 0) >= NFREQ
    to = lax.broadcasted_iota(jnp.int32, (PAIR, PAIR), 1) >= NFREQ
    matrix = jnp.where(at == to, 0.2 * both, 0.0)

    angles = lax.broadcasted_iota(jnp.int32, (40, P_DEV), 0).astype(f32) * (2.0 * jnp.pi / NDIR)
    align = jnp.maximum(jnp.cos(angles - dirs[...]), 0.0)
    growth = speed[...] * align

    place = lax.broadcasted_iota(jnp.int32, (PAIR, P_DEV), 0)
    first = place < NFREQ
    phase = (jnp.where(first, place, place - NFREQ).astype(f32) + 1.0) * (1.0 / NFREQ)

    for quad in range(4):
        begin = 2 * (QPAD * quad + 320)
        out[begin : begin + 64, :] = jnp.zeros((64, LANES), f32)

    total = jnp.zeros((8, P_DEV), f32)
    for at, copy in enumerate(loads):
        copy.wait()
        for tile in range(PART // 8):
            begin = at * PART + tile * 8
            total = total + spec[begin : begin + 8, :]
    energy = jnp.sum(total, axis=0, keepdims=True) * (1.0 / BINS)
    amp[...] = growth - 0.5 * jnp.sqrt(energy / (energy + 1.0))

    stores = []
    for pair in range(NDIR // 2):
        low = amp[2 * pair : 2 * pair + 1, :]
        high = amp[2 * pair + 1 : 2 * pair + 2, :]
        relaxed = spec[PAIR * pair : PAIR * pair + PAIR, :] * jnp.exp(phase * jnp.where(first, low, high))
        forced = relaxed + lax.dot_general(
            matrix, relaxed, (((1,), (0,)), ((), ())), precision=lax.Precision.HIGH, preferred_element_type=f32
        )
        quad_low, quad_high = (2 * pair) // 9, (2 * pair + 1) // 9
        base = PAIR * pair + (QPAD - QUAD) * quad_low
        for half in range(HALVES):
            part = forced[:, half * LANES : (half + 1) * LANES]
            if quad_low == quad_high:
                out[pl.ds(2 * base + half, PAIR, stride=2), :] = part
            else:
                other = PAIR * pair + (QPAD - QUAD) * quad_high + 32
                out[pl.ds(2 * base + half, 40, stride=2), :] = part[:40]
                out[pl.ds(2 * other + half, 40, stride=2), :] = part[32:]
        if (2 * pair + 2) // 9 > len(stores):
            rows = pl.ds(len(stores) * 2 * QPAD, 2 * QPAD)
            stores.append(pltpu.make_async_copy(out.at[rows, :], out_hbm.at[rows, :], out_sems.at[len(stores)]))
            stores[-1].start()
    for copy in stores:
        copy.wait()


def source_terms(spectrum, wind_speed, wind_dir, coupling):
    f32 = jnp.float32
    return pl.pallas_call(
        source_kernel,
        out_shape=jax.ShapeDtypeStruct((ROWS, LANES), f32),
        in_specs=[pl.BlockSpec(memory_space=pltpu.HBM)] * 4,
        out_specs=pl.BlockSpec(memory_space=pltpu.HBM),
        scratch_shapes=[
            pltpu.VMEM((BINS, P_DEV), f32),
            pltpu.VMEM((1, P_DEV), f32),
            pltpu.VMEM((1, P_DEV), f32),
            pltpu.VMEM((NFREQ, NFREQ), f32),
            pltpu.VMEM((40, P_DEV), f32),
            pltpu.VMEM((ROWS, LANES), f32),
            pltpu.SemaphoreType.DMA((PARTS + 3,)),
            pltpu.SemaphoreType.DMA((4,)),
        ],
        compiler_params=pltpu.CompilerParams(vmem_limit_bytes=63 * 1024 * 1024),
        name="source_terms",
    )(spectrum.T, wind_speed.reshape(1, P_DEV), wind_dir.reshape(1, P_DEV), coupling)


def propagate_kernel(line_ref, off_ref, end_ref, up_ref, scale_ref, recv_ref, index_ref, mask_ref, spot_ref, coef_ref, out_ref, src, dst, *bufs):
    up_y = up_ref[0]
    lane = lax.broadcasted_iota(jnp.int32, (GROUP, LANES), 1)
    edge = lane == jnp.where(up_y > 0, 0, LANES - 1)
    shift = jnp.where(up_y > 0, 1, LANES - 1)

    for slot in range(SLOTS):
        for half in range(HALVES):
            part = recv_ref[pl.ds(HALVES * slot + half, N_DEV, stride=CHUNK), :]
            src[pl.ds(half * LANES * GROUP + slot, LANES, stride=GROUP), :] = part.T * scale_ref[slot]

    for buf in bufs:
        buf[...] = jnp.zeros_like(buf)
    bufs = [bufs[2 * s : 2 * s + 2] for s in range(SUB + 1)]

    coef_x = coef_ref[0:GROUP, :]
    coef_y = coef_ref[GROUP : 2 * GROUP, :]

    def wide(ref, cell):
        return jnp.broadcast_to(ref[pl.ds(cell, 1), :], (GROUP, LANES))

    def take(values, spots):
        return lax.gather(
            values, spots[:, :, None], ALONG_LANES, slice_sizes=(1, 1), mode=lax.GatherScatterMode.PROMISE_IN_BOUNDS
        )

    def lines(begin):
        return pl.ds(pl.multiple_of(begin, GROUP), GROUP)

    def at(i, j):
        begin = (i * COLS + j) * GROUP
        return slice(begin, begin + GROUP)

    def scatter(cell, values):
        taken = take(values, wide(spot_ref, cell))
        begin = line_ref[cell]
        off = off_ref[cell]
        end = end_ref[cell]
        pltpu.store(dst.at[lines(begin), :], taken, mask=(lane >= off) & (lane < end))
        pltpu.store(dst.at[lines(begin + GROUP), :], taken, mask=lane < end - LANES)

    def gather(cell):
        begin = line_ref[cell]
        both = jnp.where(lane >= off_ref[cell], src[lines(begin), :], src[lines(begin + GROUP), :])
        return jnp.where(wide(mask_ref, cell) > 0, take(both, wide(index_ref, cell)), 0.0)

    def round_of(u, p):
        base = pl.multiple_of(u * STEP, STEP)
        above = [[bufs[step][p][at(SLAB - 1, j), :] for j in range(COLS)] for step in range(SUB)]
        for i in range(SLAB):
            if not MERGE_OUT:
                for j in range(COLS):
                    scatter(base + (i * COLS + j), bufs[SUB][1 - p][at(i, j), :])
            for step in range(SUB, 0, -1):
                fields = [bufs[step - 1][1 - p][at(i, j), :] for j in range(COLS)]
                turned = [pltpu.roll(field, shift, 1) for field in fields]
                for j in range(COLS):
                    cell = base + ((DELAY - step) * STEP + i * COLS + j)
                    upwind_y = jnp.where(edge, turned[j - 1] if j else 0.0, turned[j])
                    moved = fields[j] + (coef_x * above[step - 1][j] + coef_y * upwind_y)
                    moved = wide(mask_ref, cell) * moved
                    if step == SUB and MERGE_OUT:
                        scatter(cell, moved)
                    else:
                        bufs[step][p][at(i, j), :] = moved
                above[step - 1] = fields
            for j in range(COLS):
                bufs[0][p][at(i, j), :] = gather(base + (DELAY * STEP + i * COLS + j))

    def two_rounds(u, carry):
        round_of(2 * u, 0)
        round_of(2 * u + 1, 1)
        return carry

    lax.fori_loop(0, ROUNDS // 2, two_rounds, 0, unroll=3)

    for slot in range(SLOTS):
        for half in range(HALVES):
            part = dst[pl.ds(half * LANES * GROUP + slot, LANES, stride=GROUP), :]
            out_ref[pl.ds(HALVES * slot + half, N_DEV, stride=CHUNK), :] = part.T


def propagation_tables(land_mask, sea_index):
    f32 = jnp.float32
    dev = lax.axis_index("dev")
    quad = dev // QDEV
    within = (dev % QDEV) * SLOTS + jnp.arange(GROUP)
    bins = quad * QUAD + within
    real = (within < QUAD) & (jnp.arange(GROUP) < SLOTS)
    speeds = jnp.where(real, 0.45 * 1.1 ** (-(bins % NFREQ).astype(f32)), 0.0)
    angle = (bins // NFREQ).astype(f32) * (2.0 * jnp.pi / NDIR)
    abs_x = jnp.abs(speeds * jnp.cos(angle))
    abs_y = jnp.abs(speeds * jnp.sin(angle))
    stay = 1.0 - abs_x - abs_y
    coef = jnp.broadcast_to(jnp.concatenate([abs_x / stay, abs_y / stay])[:, None], (2 * GROUP, LANES))
    scale = stay * stay * stay * stay
    up_x = (quad == 0) | (quad == 3)
    up_y = quad < 2

    def ordered(table):
        table = table.reshape((NXG, COLS) + table.shape[1:])
        table = jnp.where(up_x, table, jnp.flip(table, 0))
        table = jnp.where(up_y, table, jnp.flip(table, 1))
        table = table.reshape((BLOCKS,) + table.shape[2:])
        return jnp.pad(table, ((DELAY * STEP, (ROUNDS - SLABS) * STEP),) + ((0, 0),) * (table.ndim - 1))

    mask = land_mask.reshape(BLOCKS, LANES).astype(f32)
    upto = jnp.dot(mask, jnp.triu(jnp.ones((LANES, LANES), f32)), preferred_element_type=f32)
    before = jnp.dot(jnp.tril(jnp.ones((BLOCKS, BLOCKS), f32), -1), upto[:, LANES - 1 :], preferred_element_type=f32)
    index = (before + upto - mask).astype(jnp.int32) & (LANES - 1)
    start = before[:, 0].astype(jnp.int32)
    line = start >> 7
    off = start & (LANES - 1)
    end = off + upto[:, LANES - 1].astype(jnp.int32)

    spot = (sea_index & (LANES - 1)).reshape(N_DEV, P_DEV).T.astype(f32)
    lines = jnp.arange(P_DEV)
    one = jnp.dot((line[:, None] == lines).astype(f32), spot, preferred_element_type=f32)
    two = jnp.dot((line[:, None] + 1 == lines).astype(f32), spot, preferred_element_type=f32)
    spots = jnp.where(jnp.arange(LANES) >= off[:, None], one, two).astype(jnp.int32)

    scalars = [ordered(line * GROUP), ordered(off), ordered(end), up_y.astype(jnp.int32)[None], scale]
    return scalars, [ordered(index), ordered(mask), ordered(spots), coef]


def propagate(recv, scalars, vectors):
    f32 = jnp.float32
    return pl.pallas_call(
        propagate_kernel,
        out_shape=jax.ShapeDtypeStruct((ROWS, LANES), f32),
        in_specs=[pl.BlockSpec(memory_space=pltpu.SMEM)] * 5 + [pl.BlockSpec(memory_space=pltpu.VMEM)] * 5,
        out_specs=pl.BlockSpec(memory_space=pltpu.VMEM),
        scratch_shapes=[pltpu.VMEM(((P_DEV + 2) * GROUP, LANES), f32)] * 2
        + [pltpu.VMEM((SLAB * COLS * GROUP, LANES), f32)] * (2 * (SUB + 1)),
        compiler_params=pltpu.CompilerParams(vmem_limit_bytes=VMEM),
        name="propagate",
    )(*scalars, recv, *vectors)


def collect_kernel(in_ref, out_ref):
    for quad in (1, 0, 3, 2):
        lead = 4 * (quad % 2)
        for half in range(HALVES):
            part = in_ref[pl.ds(2 * (QPAD * quad - lead) + half, QUAD + lead, stride=2), :]
            out_ref[QUAD * quad - lead : QUAD * (quad + 1), half * LANES : (half + 1) * LANES] = part


def collect(back):
    return pl.pallas_call(
        collect_kernel,
        out_shape=jax.ShapeDtypeStruct((BINS, P_DEV), jnp.float32),
        in_specs=[pl.BlockSpec(memory_space=pltpu.VMEM)],
        out_specs=pl.BlockSpec(memory_space=pltpu.VMEM),
        compiler_params=pltpu.CompilerParams(vmem_limit_bytes=VMEM),
        name="collect",
    )(back)


def exchange(rows):
    swapped = lax.all_to_all(rows.reshape(ROWS, 1, LANES), "dev", split_axis=0, concat_axis=0, tiled=True)
    return swapped.reshape(ROWS, LANES)


def on_device(spectrum, wind_speed, wind_dir, coupling, land_mask, sea_index):
    sent = source_terms(spectrum, wind_speed, wind_dir, coupling)
    moved = propagate(exchange(sent), *propagation_tables(land_mask, sea_index))
    return collect(exchange(moved)).T


def solution(mesh):
    in_specs = (P("dev", None), P("dev"), P("dev"), P(), P(), P())
    return jax.shard_map(on_device, mesh=mesh, in_specs=in_specs, out_specs=P("dev", None), check_vma=False)
```

time: 84.2 us -> 78.4 us (0.931)
  waiting for transfers between devices: 22.1 us -> 19.4 us
  Pallas kernels: 17.8 us -> 15.4 us
  local copies, waits for them, and re-layouts: 3.88 us -> 2.17 us
    unnamed x12 -> x4, local copies, waits for them, and re-layouts: 3.42 us -> 0.01 us
    all_to_all x1, waiting for transfers between devices: 22.1 us -> 19.4 us  [exchange(): lax.all_to_all(rows.reshape(ROWS, 1, LANES), 'dev', split_axis=0, concat_...]
    pallas_call x1, Pallas kernels: 13.8 us -> 11.2 us  [propagate(): pl.pallas_call(propagate_kernel, out_shape=jax.ShapeDtypeStruct((ROWS, LA...]
    rev x0 -> x7, local copies, waits for them, and re-layouts: none -> 0.92 us  [the longest x6 0.91 us: ordered(): table = jnp.where(up_y, table, jnp.flip(table, 1))]
  transfers between devices with their start and end apart: 1 -> 1, of which waited for: 1 -> 1; matrix products, arithmetic and copies ran while one was open for 2% -> 5% of each run, Pallas kernels for 0% -> 0%
where the time goes in v2:
time: 78.4 us; the launch traced here: 78.1 us
  blocking collectives  27.6 us (35%)
  waiting for transfers between devices  19.4 us (25%)
  Pallas kernels  15.4 us (20%)
  starting transfers between devices  11.5 us (15%)
  local copies, waits for them, and re-layouts  2.17 us (3%)
  matrix products  1.09 us (1%)
    all_to_all x1, blocking collectives, exchange(): lax.all_to_all(rows.reshape(ROWS, 1, LANES), 'dev', split_axis=0, concat_...  27.6 us
    all_to_all x1, waiting for transfers between devices, exchange(): lax.all_to_all(rows.reshape(ROWS, 1, LANES), 'dev', split_axis=0, concat_...  19.4 us
    all_to_all x1, starting transfers between devices, exchange(): lax.all_to_all(rows.reshape(ROWS, 1, LANES), 'dev', split_axis=0, concat_...  11.5 us
    pallas_call x1, Pallas kernels, propagate(): pl.pallas_call(propagate_kernel, out_shape=jax.ShapeDtypeStruct((ROWS, LA...  11.2 us
    pallas_call x1, Pallas kernels, source_terms(): pl.pallas_call(source_kernel, out_shape=jax.ShapeDtypeStruct((ROWS, LANES...  3.13 us
  transfers between devices with their start and end apart: 1, of which 1 were waited for; matrix products, arithmetic and copies ran while one was open for 5% of the time, Pallas kernels for 0%

profile of v2, /device:TPU:1, one launch (start us, length us, event | category | flops | bytes accessed | tf_op | source)
XLA Modules:
  0.0 78.1 jit_solution(18405320959054576009)
XLA Ops:
  0.0 3.1 %source_terms.1 = f32[2816,128]{1,0:T(8,128)} custom-call(f32[1296,256]{1,0:T(8,128)} %bitcast.35, f32[1,256]{1,0:T(1,128)} %bitcast.43, f32[1,256]{1,0:T(1,128)} %bitcast.44, f32[36,36]{1,0:T(8,128)} %coupling_hbm.1), custom_call_target="tpu_custom_call" | custom-call | tf_op jit(solution)/shard_map/source_terms/pallas_call | solution.py:121
  3.1 0.0 copy-start
  3.2 11.5 %all-to-all-start = ((f32[2816,1,128]{2,1,0:T(1,128)}), f32[2816,1,128]{2,1,0:T(1,128)S(1)}, u32[]{:S(2)}, u32[]{:S(2)}) async-start(f32[2816,1,128]{2,1,0:T(1,128)} %bitcast.32), calls=%async_computation | async-start | bytes 2883584 | tf_op jit(solution)/shard_map/all_to_all | solution.py:300
  14.7 0.0 copy-done
  14.8 0.3 convolution_bitcast_fusion
  15.1 0.0 copy-start.1
  15.1 0.3 convolution_reduce_fusion
  15.4 0.1 copy.12
  15.5 0.1 convert_element_type.63
  15.6 0.1 convert_element_type.57
  15.8 0.1 convert_element_type.59
  15.9 0.1 rev.43
  16.0 0.1 reshape.77
  16.1 0.1 pad.21.line_ref
  16.2 0.1 rev.45
  16.3 0.1 reshape.78
  16.4 0.1 pad.22.off_ref
  16.5 0.1 rev.47
  16.6 0.1 reshape.79
  16.7 0.1 pad.23.end_ref
  16.7 0.0 copy-done.1
  16.8 0.1 copy.13
  17.0 0.2 fusion.2
  17.2 0.3 fusion
  17.5 0.1 reverse_select_fusion
  17.6 0.2 rev.49
  17.9 0.2 rev.51
  18.2 0.2 rev.53
  18.5 0.1 broadcast_select_fusion.1
  18.5 0.1 multiply_multiply_fusion.scale_ref
  18.6 0.1 fusion.19
  18.7 0.1 pad_maximum_fusion
  18.8 19.4 %all-to-all-done = f32[2816,1,128]{2,1,0:T(1,128)S(1)} async-done(((f32[2816,1,128]{2,1,0:T(1,128)}), f32[2816,1,128]{2,1,0:T(1,128)S(1)}, u32[]{:S(2)}, u32[]{:S(2)}) %all-to-all-start) | async-done | bytes 1441824 | tf_op jit(solution)/shard_map/all_to_all | solution.py:300
  38.2 0.1 broadcast_in_dim.42.coef_ref
  38.3 11.2 %propagate.1 = f32[2816,128]{1,0:T(8,128)S(1)} custom-call(s32[472]{0:T(512)S(1)} %pad.21.line_ref, s32[472]{0:T(512)S(1)} %pad.22.off_ref, s32[472]{0:T(512)S(1)} %pad.23.end_ref, s32[1]{0:T(128)} %bitcast.1.up_ref, f32[16]{0:T(128)S(1)} %multiply_multiply_fusion.scale_ref, f32[2816,128]{1,0:T(8,128)S(1)} %bitcast.30, s32[472,128]{1,0:T(8,128)S(1)} %pad.24.index_ref, ...), custom_call_target="tpu_custom_call" | custom-call | tf_op jit(solution)/shard_map/propagate/pallas_call | solution.py:268
  49.4 27.6 %all_to_all.10 = f32[2816,1,128]{2,1,0:T(1,128)S(1)} all-to-all(f32[2816,1,128]{2,1,0:T(1,128)S(1)} %bitcast.31), channel_id=1, replica_groups=mesh['dev'=128] {'dev'}, dimensions={0} | all-to-all | bytes 2883584 | tf_op jit(solution)/shard_map/all_to_all | solution.py:300
  77.0 1.1 %collect.1 = f32[1296,256]{1,0:T(8,128)} custom-call(f32[2816,128]{1,0:T(8,128)S(1)} %bitcast.29), custom_call_target="tpu_custom_call" | custom-call | tf_op jit(solution)/shard_map/collect/pallas_call | solution.py:289
  (22 shorter events, 0.4 us)
Async XLA Ops:
  3.1 11.6 %copy-start = (s32[96,512]{1,0:T(8,128)S(1)}, s32[96,512]{1,0:T(8,128)}, u32[]{:S(2)}) copy-start(s32[96,512]{1,0:T(8,128)} %param.10) | copy-start | bytes 589828
  3.2 35.0 %all-to-all-start = ((f32[2816,1,128]{2,1,0:T(1,128)}), f32[2816,1,128]{2,1,0:T(1,128)S(1)}, u32[]{:S(2)}, u32[]{:S(2)}) async-start(f32[2816,1,128]{2,1,0:T(1,128)} %bitcast.32), calls=%async_computation | async-start | bytes 2883584 | tf_op jit(solution)/shard_map/all_to_all | solution.py:300
  15.1 1.7 %copy-start.1 = (s32[32768]{0:T(1024)S(1)}, s32[32768]{0:T(1024)}, u32[]{:S(2)}) copy-start(s32[32768]{0:T(1024)} %param.11) | copy-start | bytes 393220

commit v3 on v2

--- a/solution.py
+++ b/solution.py
@@ -18,11 +18,13 @@
 BLOCKS = NXG * COLS
 QUAD = BINS // 4
 QDEV = N_DEV // 4
-SLOTS = -(-QUAD // QDEV)
-QPAD = SLOTS * QDEV
+SLOTS = QUAD // QDEV
+REST = QUAD - SLOTS * QDEV
+WINDOWS = 3
+OWNED = (0, 100, 160, 256)
 GROUP = 16
 HALVES = P_DEV // LANES
-CHUNK = SLOTS * HALVES
+CHUNK = SLOTS * HALVES + 1
 ROWS = N_DEV * CHUNK
 PAIR = 2 * NFREQ
 PARTS = 6
@@ -43,6 +45,10 @@
 VMEM = 48 * 1024 * 1024
 
 
+def first_bin(quad):
+    return QUAD * quad + REST * (quad % 2)
+
+
 def source_kernel(spec_hbm, speed_hbm, dir_hbm, coupling_hbm, out_hbm, spec, speed, dirs, coupling, amp, out, in_sems, out_sems):
     f32 = jnp.float32
     small = [
@@ -77,9 +83,11 @@
     first = place < NFREQ
     phase = (jnp.where(first, place, place - NFREQ).astype(f32) + 1.0) * (1.0 / NFREQ)
 
+    lane = lax.broadcasted_iota(jnp.int32, (8, LANES), 1)
+    unused = QDEV - REST * WINDOWS
     for quad in range(4):
-        begin = 2 * (QPAD * quad + 320)
-        out[begin : begin + 64, :] = jnp.zeros((64, LANES), f32)
+        begin = (QDEV * (quad + 1) - unused) * CHUNK + CHUNK - 1
+        out[pl.ds(begin, unused, stride=CHUNK), :] = jnp.zeros((unused, LANES), f32)
 
     total = jnp.zeros((8, P_DEV), f32)
     for at, copy in enumerate(loads):
@@ -98,18 +106,25 @@
         forced = relaxed + lax.dot_general(
             matrix, relaxed, (((1,), (0,)), ((), ())), precision=lax.Precision.HIGH, preferred_element_type=f32
         )
-        quad_low, quad_high = (2 * pair) // 9, (2 * pair + 1) // 9
-        base = PAIR * pair + (QPAD - QUAD) * quad_low
-        for half in range(HALVES):
-            part = forced[:, half * LANES : (half + 1) * LANES]
-            if quad_low == quad_high:
-                out[pl.ds(2 * base + half, PAIR, stride=2), :] = part
+        for tile in range(PAIR // 8):
+            begin = PAIR * pair + tile * 8
+            halves = [forced[tile * 8 : tile * 8 + 8, half * LANES : (half + 1) * LANES] for half in range(HALVES)]
+            if begin % (2 * QUAD) == QUAD - REST:
+                turned = [pltpu.roll(half, LANES // 2, 1) for half in halves]
+                windows = (halves[0], jnp.where(lane < LANES // 2, turned[0], turned[1]), halves[1])
+                for at in range(2):
+                    for window in range(WINDOWS):
+                        first_row = ((begin // QUAD + at) * QDEV + window) * CHUNK + CHUNK - 1
+                        rows = pl.ds(first_row, REST, stride=WINDOWS * CHUNK)
+                        out[rows, :] = windows[window][at * REST : (at + 1) * REST]
             else:
-                other = PAIR * pair + (QPAD - QUAD) * quad_high + 32
-                out[pl.ds(2 * base + half, 40, stride=2), :] = part[:40]
-                out[pl.ds(2 * other + half, 40, stride=2), :] = part[32:]
+                quad = begin // QUAD
+                slot, member = divmod(begin - first_bin(quad), QDEV)
+                for half in range(HALVES):
+                    first_row = (quad * QDEV + member) * CHUNK + HALVES * slot + half
+                    out[pl.ds(first_row, 8, stride=CHUNK), :] = halves[half]
         if (2 * pair + 2) // 9 > len(stores):
-            rows = pl.ds(len(stores) * 2 * QPAD, 2 * QPAD)
+            rows = pl.ds(len(stores) * QDEV * CHUNK, QDEV * CHUNK)
             stores.append(pltpu.make_async_copy(out.at[rows, :], out_hbm.at[rows, :], out_sems.at[len(stores)]))
             stores[-1].start()
     for copy in stores:
@@ -144,10 +159,11 @@
     edge = lane == jnp.where(up_y > 0, 0, LANES - 1)
     shift = jnp.where(up_y > 0, 1, LANES - 1)
 
-    for slot in range(SLOTS):
-        for half in range(HALVES):
-            part = recv_ref[pl.ds(HALVES * slot + half, N_DEV, stride=CHUNK), :]
-            src[pl.ds(half * LANES * GROUP + slot, LANES, stride=GROUP), :] = part.T * scale_ref[slot]
+    pieces = [(HALVES * slot + half, slot, half * LANES * GROUP) for slot in range(SLOTS) for half in range(HALVES)]
+    pieces.append((CHUNK - 1, SLOTS, up_ref[1] * (LANES // 2 * GROUP)))
+    for row, slot, begin in pieces:
+        part = recv_ref[pl.ds(row, N_DEV, stride=CHUNK), :]
+        src[pl.ds(begin + slot, LANES, stride=GROUP), :] = part.T * scale_ref[slot]
 
     for buf in bufs:
         buf[...] = jnp.zeros_like(buf)
@@ -214,19 +230,22 @@
 
     lax.fori_loop(0, ROUNDS // 2, two_rounds, 0, unroll=3)
 
-    for slot in range(SLOTS):
-        for half in range(HALVES):
-            part = dst[pl.ds(half * LANES * GROUP + slot, LANES, stride=GROUP), :]
-            out_ref[pl.ds(HALVES * slot + half, N_DEV, stride=CHUNK), :] = part.T
+    for row, slot, begin in pieces:
+        part = dst[pl.ds(begin + slot, LANES, stride=GROUP), :]
+        out_ref[pl.ds(row, N_DEV, stride=CHUNK), :] = part.T
 
 
 def propagation_tables(land_mask, sea_index):
     f32 = jnp.float32
     dev = lax.axis_index("dev")
     quad = dev // QDEV
-    within = (dev % QDEV) * SLOTS + jnp.arange(GROUP)
-    bins = quad * QUAD + within
-    real = (within < QUAD) & (jnp.arange(GROUP) < SLOTS)
+    member = dev % QDEV
+    slots = jnp.arange(GROUP)
+    odd = quad % 2
+    whole = quad * QUAD + REST * odd + QDEV * slots + member
+    rest = quad * QUAD + (QUAD - REST) * (1 - odd) + member // WINDOWS
+    bins = jnp.where(slots < SLOTS, whole, rest)
+    real = (slots < SLOTS) | ((slots == SLOTS) & (member < REST * WINDOWS))
     speeds = jnp.where(real, 0.45 * 1.1 ** (-(bins % NFREQ).astype(f32)), 0.0)
     angle = (bins // NFREQ).astype(f32) * (2.0 * jnp.pi / NDIR)
     abs_x = jnp.abs(speeds * jnp.cos(angle))
@@ -259,7 +278,7 @@
     two = jnp.dot((line[:, None] + 1 == lines).astype(f32), spot, preferred_element_type=f32)
     spots = jnp.where(jnp.arange(LANES) >= off[:, None], one, two).astype(jnp.int32)
 
-    scalars = [ordered(line * GROUP), ordered(off), ordered(end), up_y.astype(jnp.int32)[None], scale]
+    scalars = [ordered(line * GROUP), ordered(off), ordered(end), jnp.stack([up_y.astype(jnp.int32), member % WINDOWS]), scale]
     return scalars, [ordered(index), ordered(mask), ordered(spots), coef]
 
 
@@ -278,11 +297,22 @@
 
 
 def collect_kernel(in_ref, out_ref):
-    for quad in (1, 0, 3, 2):
-        lead = 4 * (quad % 2)
+    lane = lax.broadcasted_iota(jnp.int32, (REST, LANES), 1)
+    for quad in range(4):
         for half in range(HALVES):
-            part = in_ref[pl.ds(2 * (QPAD * quad - lead) + half, QUAD + lead, stride=2), :]
-            out_ref[QUAD * quad - lead : QUAD * (quad + 1), half * LANES : (half + 1) * LANES] = part
+            columns = slice(half * LANES, (half + 1) * LANES)
+            for slot in range(SLOTS):
+                part = in_ref[pl.ds(quad * QDEV * CHUNK + HALVES * slot + half, QDEV, stride=CHUNK), :]
+                begin = first_bin(quad) + QDEV * slot
+                out_ref[begin : begin + QDEV, columns] = part
+        begin = QUAD * quad + (0 if quad % 2 else QUAD - REST)
+        low, middle, high = [
+            in_ref[pl.ds((quad * QDEV + window) * CHUNK + CHUNK - 1, REST, stride=WINDOWS * CHUNK), :]
+            for window in range(WINDOWS)
+        ]
+        middle = pltpu.roll(middle, LANES // 2, 1)
+        out_ref[begin : begin + REST, :LANES] = jnp.where(lane < OWNED[1], low, middle)
+        out_ref[begin : begin + REST, LANES:] = jnp.where(lane < OWNED[2] - LANES, middle, high)
 
 
 def collect(back):

time: 78.4 us -> 76.9 us (0.981)
  no operation moved by 1% of the time
where the time goes in v3:
time: 76.9 us; the launch traced here: 76.7 us
  blocking collectives  26.9 us (35%)
  waiting for transfers between devices  18.7 us (24%)
  Pallas kernels  15.3 us (20%)
  starting transfers between devices  11.5 us (15%)
  local copies, waits for them, and re-layouts  2.18 us (3%)
  matrix products  1.09 us (1%)
    all_to_all x1, blocking collectives, exchange(): lax.all_to_all(rows.reshape(ROWS, 1, LANES), 'dev', split_axis=0, concat_...  26.9 us
    all_to_all x1, waiting for transfers between devices, exchange(): lax.all_to_all(rows.reshape(ROWS, 1, LANES), 'dev', split_axis=0, concat_...  18.7 us
    all_to_all x1, starting transfers between devices, exchange(): lax.all_to_all(rows.reshape(ROWS, 1, LANES), 'dev', split_axis=0, concat_...  11.5 us
    pallas_call x1, Pallas kernels, propagate(): pl.pallas_call(propagate_kernel, out_shape=jax.ShapeDtypeStruct((ROWS, LA...  11 us
    pallas_call x1, Pallas kernels, source_terms(): pl.pallas_call(source_kernel, out_shape=jax.ShapeDtypeStruct((ROWS, LANES...  3.18 us
  transfers between devices with their start and end apart: 1, of which 1 were waited for; matrix products, arithmetic and copies ran while one was open for 5% of the time, Pallas kernels for 0%

profile of v3, /device:TPU:1, one launch (start us, length us, event | category | flops | bytes accessed | tf_op | source)
XLA Modules:
  0.0 76.7 jit_solution(17893229558999971257)
XLA Ops:
  0.0 3.2 %source_terms.1 = f32[2688,128]{1,0:T(8,128)} custom-call(f32[1296,256]{1,0:T(8,128)} %bitcast.36, f32[1,256]{1,0:T(1,128)} %bitcast.44, f32[1,256]{1,0:T(1,128)} %bitcast.45, f32[36,36]{1,0:T(8,128)} %coupling_hbm.1), custom_call_target="tpu_custom_call" | custom-call | tf_op jit(solution)/shard_map/source_terms/pallas_call | solution.py:136
  3.2 0.0 copy-start
  3.2 11.5 %all-to-all-start = ((f32[2688,1,128]{2,1,0:T(1,128)}), f32[2688,1,128]{2,1,0:T(1,128)S(1)}, u32[]{:S(2)}, u32[]{:S(2)}) async-start(f32[2688,1,128]{2,1,0:T(1,128)} %bitcast.33), calls=%async_computation | async-start | bytes 2752512 | tf_op jit(solution)/shard_map/all_to_all | solution.py:330
  14.7 0.0 copy-done
  14.8 0.0 copy-start.1
  14.8 0.3 convolution_bitcast_fusion
  15.1 0.3 convolution_reduce_fusion
  15.4 0.1 copy.12
  15.6 0.1 convert_element_type.57
  15.7 0.1 convert_element_type.59
  15.9 0.1 rev.43
  16.0 0.1 rev.45
  16.1 0.1 rev.47
  16.2 0.0 copy-done.1
  16.3 0.1 copy.13
  16.4 0.2 fusion.2
  16.6 0.3 fusion
  16.9 0.1 reverse_select_fusion
  17.0 0.2 rev.49
  17.3 0.1 convert_element_type.63
  17.4 0.1 reshape.77
  17.5 0.1 pad.21.line_ref
  17.6 0.1 reshape.78
  17.7 0.1 pad.22.off_ref
  17.8 0.1 reshape.79
  17.9 0.1 pad.23.end_ref
  18.0 0.2 rev.51
  18.3 0.2 rev.53
  18.6 0.1 broadcast_select_fusion.1
  18.7 0.1 pad_add_fusion.up_ref
  18.7 0.1 fusion.22
  18.8 0.1 pad_maximum_fusion
  18.9 18.7 %all-to-all-done = f32[2688,1,128]{2,1,0:T(1,128)S(1)} async-done(((f32[2688,1,128]{2,1,0:T(1,128)}), f32[2688,1,128]{2,1,0:T(1,128)S(1)}, u32[]{:S(2)}, u32[]{:S(2)}) %all-to-all-start) | async-done | bytes 1376288 | tf_op jit(solution)/shard_map/all_to_all | solution.py:330
  37.6 0.1 broadcast_in_dim.40.coef_ref
  37.6 11.0 %propagate.1 = f32[2688,128]{1,0:T(8,128)S(1)} custom-call(s32[472]{0:T(512)S(1)} %pad.21.line_ref, s32[472]{0:T(512)S(1)} %pad.22.off_ref, s32[472]{0:T(512)S(1)} %pad.23.end_ref, s32[2]{0:T(128)S(1)} %pad_add_fusion.up_ref, f32[16]{0:T(128)S(1)} %get-tuple-element.15.scale_ref, f32[2688,128]{1,0:T(8,128)S(1)} %bitcast.30, s32[472,128]{1,0:T(8,128)S(1)} %pad.24.index_ref, ...), custom_call_target="tpu_custom_call" | custom-call | tf_op jit(solution)/shard_map/propagate/pallas_call | solution.py:287
  48.6 26.9 %all_to_all.10 = f32[2688,1,128]{2,1,0:T(1,128)S(1)} all-to-all(f32[2688,1,128]{2,1,0:T(1,128)S(1)} %bitcast.31), channel_id=1, replica_groups=mesh['dev'=128] {'dev'}, dimensions={0} | all-to-all | bytes 2752512 | tf_op jit(solution)/shard_map/all_to_all | solution.py:330
  75.5 1.2 %collect.1 = f32[1296,256]{1,0:T(8,128)} custom-call(f32[2688,128]{1,0:T(8,128)S(1)} %bitcast.32), custom_call_target="tpu_custom_call" | custom-call | tf_op jit(solution)/shard_map/collect/pallas_call | solution.py:319
  (23 shorter events, 0.4 us)
Async XLA Ops:
  3.2 11.6 %copy-start = (s32[96,512]{1,0:T(8,128)S(1)}, s32[96,512]{1,0:T(8,128)}, u32[]{:S(2)}) copy-start(s32[96,512]{1,0:T(8,128)} %param.10) | copy-start | bytes 589828
  3.2 34.4 %all-to-all-start = ((f32[2688,1,128]{2,1,0:T(1,128)}), f32[2688,1,128]{2,1,0:T(1,128)S(1)}, u32[]{:S(2)}, u32[]{:S(2)}) async-start(f32[2688,1,128]{2,1,0:T(1,128)} %bitcast.33), calls=%async_computation | async-start | bytes 2752512 | tf_op jit(solution)/shard_map/all_to_all | solution.py:330
  14.8 1.4 %copy-start.1 = (s32[32768]{0:T(1024)S(1)}, s32[32768]{0:T(1024)}, u32[]{:S(2)}) copy-start(s32[32768]{0:T(1024)} %param.11) | copy-start | bytes 393220

commit v4 on v3

--- a/solution.py
+++ b/solution.py
@@ -22,7 +22,9 @@
 REST = QUAD - SLOTS * QDEV
 WINDOWS = 3
 OWNED = (0, 100, 160, 256)
-GROUP = 16
+GROUP = 8
+HALF = GROUP // 2
+HELD = 2 * GROUP
 HALVES = P_DEV // LANES
 CHUNK = SLOTS * HALVES + 1
 ROWS = N_DEV * CHUNK
@@ -32,9 +34,7 @@
 SLAB = 2
 SLABS = NXG // SLAB
 STEP = SLAB * COLS
-MERGE_OUT = False
-DELAY = SUB if MERGE_OUT else SUB + 1
-ROUNDS = -(-(SLABS + DELAY) // 2) * 2
+UNROLL = 14
 ALONG_LANES = lax.GatherDimensionNumbers(
     offset_dims=(),
     collapsed_slice_dims=(1,),
@@ -153,27 +153,37 @@
     )(spectrum.T, wind_speed.reshape(1, P_DEV), wind_dir.reshape(1, P_DEV), coupling)
 
 
-def propagate_kernel(line_ref, off_ref, end_ref, up_ref, scale_ref, recv_ref, index_ref, mask_ref, spot_ref, coef_ref, out_ref, src, dst, *bufs):
+def propagate_kernel(
+    line_ref, off_ref, end_ref, up_ref, scale_ref, recv_ref, index_ref, mask_ref, spot_ref, coef_ref, out_ref, *scratch
+):
+    src, dst, src_rest, dst_rest, *bufs = scratch
     up_y = up_ref[0]
     lane = lax.broadcasted_iota(jnp.int32, (GROUP, LANES), 1)
+    low = lax.broadcasted_iota(jnp.int32, (GROUP, LANES), 0) < HALF
     edge = lane == jnp.where(up_y > 0, 0, LANES - 1)
     shift = jnp.where(up_y > 0, 1, LANES - 1)
 
     pieces = [(HALVES * slot + half, slot, half * LANES * GROUP) for slot in range(SLOTS) for half in range(HALVES)]
     pieces.append((CHUNK - 1, SLOTS, up_ref[1] * (LANES // 2 * GROUP)))
     for row, slot, begin in pieces:
-        part = recv_ref[pl.ds(row, N_DEV, stride=CHUNK), :]
-        src[pl.ds(begin + slot, LANES, stride=GROUP), :] = part.T * scale_ref[slot]
+        part = recv_ref[pl.ds(row, N_DEV, stride=CHUNK), :].T * scale_ref[slot]
+        if slot < GROUP:
+            src[pl.ds(begin + slot, LANES, stride=GROUP), :] = part
+        else:
+            src_rest[pl.ds(begin + slot - GROUP, LANES, stride=GROUP), :] = part
+            src_rest[pl.ds(begin + slot - GROUP + HALF, LANES, stride=GROUP), :] = part
 
     for buf in bufs:
         buf[...] = jnp.zeros_like(buf)
+    bufs_rest = [bufs[2 * s : 2 * s + 2] for s in range(SUB + 1, 2 * SUB + 2)]
     bufs = [bufs[2 * s : 2 * s + 2] for s in range(SUB + 1)]
-
-    coef_x = coef_ref[0:GROUP, :]
-    coef_y = coef_ref[GROUP : 2 * GROUP, :]
+    coef_x, coef_y, rest_x, rest_y = [coef_ref[k * GROUP : (k + 1) * GROUP, :] for k in range(4)]
 
     def wide(ref, cell):
         return jnp.broadcast_to(ref[pl.ds(cell, 1), :], (GROUP, LANES))
+
+    def two(ref, cell):
+        return jnp.where(low, wide(ref, cell), wide(ref, cell + 2))
 
     def take(values, spots):
         return lax.gather(
@@ -183,55 +193,93 @@
     def lines(begin):
         return pl.ds(pl.multiple_of(begin, GROUP), GROUP)
 
-    def at(i, j):
-        begin = (i * COLS + j) * GROUP
+    def at(i, j, blocks=COLS):
+        begin = (i * blocks + j) * GROUP
         return slice(begin, begin + GROUP)
 
-    def scatter(cell, values):
-        taken = take(values, wide(spot_ref, cell))
+    def store(target, cell, taken):
         begin = line_ref[cell]
         off = off_ref[cell]
         end = end_ref[cell]
-        pltpu.store(dst.at[lines(begin), :], taken, mask=(lane >= off) & (lane < end))
-        pltpu.store(dst.at[lines(begin + GROUP), :], taken, mask=lane < end - LANES)
+        pltpu.store(target.at[lines(begin), :], taken, mask=(lane >= off) & (lane < end))
+        pltpu.store(target.at[lines(begin + GROUP), :], taken, mask=lane < end - LANES)
+
+    def scatter(cell, values):
+        store(dst, cell, take(values, wide(spot_ref, cell)))
+
+    def scatter_rest(cell, values):
+        taken = take(values, two(spot_ref, cell))
+        store(dst_rest, cell, taken)
+        store(dst_rest, cell + 2, pltpu.roll(taken, HALF, 0))
 
     def gather(cell):
         begin = line_ref[cell]
         both = jnp.where(lane >= off_ref[cell], src[lines(begin), :], src[lines(begin + GROUP), :])
         return jnp.where(wide(mask_ref, cell) > 0, take(both, wide(index_ref, cell)), 0.0)
 
+    def gather_rest(cell):
+        begin, other = line_ref[cell], line_ref[cell + 2]
+        one = jnp.where(low, src_rest[lines(begin), :], src_rest[lines(other), :])
+        next_one = jnp.where(low, src_rest[lines(begin + GROUP), :], src_rest[lines(other + GROUP), :])
+        both = jnp.where(lane >= jnp.where(low, off_ref[cell], off_ref[cell + 2]), one, next_one)
+        return jnp.where(two(mask_ref, cell) > 0, take(both, two(index_ref, cell)), 0.0)
+
+    def turn(fields):
+        return [pltpu.roll(field, shift, 1) for field in fields]
+
     def round_of(u, p):
-        base = pl.multiple_of(u * STEP, STEP)
-        above = [[bufs[step][p][at(SLAB - 1, j), :] for j in range(COLS)] for step in range(SUB)]
+        def has(delay):
+            return not isinstance(u, int) or 0 <= u - delay < SLABS
+
+        def cell_of(delay, i, j):
+            return pl.multiple_of((u - delay) * STEP, STEP) + (i * COLS + j)
+
+        steps = [step for step in range(SUB, 0, -1) if has(step)]
+        above = {step: [bufs[step - 1][p][at(SLAB - 1, j), :] for j in range(COLS)] for step in steps}
+        above_rest = {step: [bufs_rest[step - 1][p][at(SLAB - 1, j, 2), :] for j in range(2)] for step in steps}
         for i in range(SLAB):
-            if not MERGE_OUT:
+            if has(SUB + 1):
                 for j in range(COLS):
-                    scatter(base + (i * COLS + j), bufs[SUB][1 - p][at(i, j), :])
-            for step in range(SUB, 0, -1):
+                    scatter(cell_of(SUB + 1, i, j), bufs[SUB][1 - p][at(i, j), :])
+                for j in range(2):
+                    scatter_rest(cell_of(SUB + 1, i, j), bufs_rest[SUB][1 - p][at(i, j, 2), :])
+            for step in steps:
                 fields = [bufs[step - 1][1 - p][at(i, j), :] for j in range(COLS)]
-                turned = [pltpu.roll(field, shift, 1) for field in fields]
+                turned = turn(fields)
                 for j in range(COLS):
-                    cell = base + ((DELAY - step) * STEP + i * COLS + j)
                     upwind_y = jnp.where(edge, turned[j - 1] if j else 0.0, turned[j])
-                    moved = fields[j] + (coef_x * above[step - 1][j] + coef_y * upwind_y)
-                    moved = wide(mask_ref, cell) * moved
-                    if step == SUB and MERGE_OUT:
-                        scatter(cell, moved)
-                    else:
-                        bufs[step][p][at(i, j), :] = moved
-                above[step - 1] = fields
-            for j in range(COLS):
-                bufs[0][p][at(i, j), :] = gather(base + (DELAY * STEP + i * COLS + j))
-
-    def two_rounds(u, carry):
-        round_of(2 * u, 0)
-        round_of(2 * u + 1, 1)
+                    moved = fields[j] + (coef_x * above[step][j] + coef_y * upwind_y)
+                    bufs[step][p][at(i, j), :] = wide(mask_ref, cell_of(step, i, j)) * moved
+                above[step] = fields
+                fields = [bufs_rest[step - 1][1 - p][at(i, j, 2), :] for j in range(2)]
+                turned = turn(fields)
+                before = jnp.where(low, 0.0, pltpu.roll(turned[1], HALF, 0))
+                for j in range(2):
+                    upwind_y = jnp.where(edge, turned[0] if j else before, turned[j])
+                    moved = fields[j] + (rest_x * above_rest[step][j] + rest_y * upwind_y)
+                    bufs_rest[step][p][at(i, j, 2), :] = two(mask_ref, cell_of(step, i, j)) * moved
+                above_rest[step] = fields
+            if has(0):
+                for j in range(COLS):
+                    bufs[0][p][at(i, j), :] = gather(cell_of(0, i, j))
+                for j in range(2):
+                    bufs_rest[0][p][at(i, j, 2), :] = gather_rest(cell_of(0, i, j))
+
+    def rounds(u, carry):
+        for k in range(UNROLL):
+            round_of(SUB + 1 + u * UNROLL + k, (SUB + 1 + k) % 2)
         return carry
 
-    lax.fori_loop(0, ROUNDS // 2, two_rounds, 0, unroll=3)
+    loops = (SLABS - SUB - 1) // UNROLL
+    for u in range(SUB + 1):
+        round_of(u, u % 2)
+    lax.fori_loop(0, loops, rounds, 0)
+    for u in range(SUB + 1 + loops * UNROLL, SLABS + SUB + 1):
+        round_of(u, u % 2)
 
     for row, slot, begin in pieces:
-        part = dst[pl.ds(begin + slot, LANES, stride=GROUP), :]
+        lines_of = dst if slot < GROUP else dst_rest
+        part = lines_of[pl.ds(begin + slot % GROUP, LANES, stride=GROUP), :]
         out_ref[pl.ds(row, N_DEV, stride=CHUNK), :] = part.T
 
 
@@ -240,18 +288,21 @@
     dev = lax.axis_index("dev")
     quad = dev // QDEV
     member = dev % QDEV
-    slots = jnp.arange(GROUP)
+    slots = jnp.arange(HELD)
     odd = quad % 2
     whole = quad * QUAD + REST * odd + QDEV * slots + member
-    rest = quad * QUAD + (QUAD - REST) * (1 - odd) + member // WINDOWS
-    bins = jnp.where(slots < SLOTS, whole, rest)
+    left = quad * QUAD + (QUAD - REST) * (1 - odd) + member // WINDOWS
+    bins = jnp.where(slots < SLOTS, whole, left)
     real = (slots < SLOTS) | ((slots == SLOTS) & (member < REST * WINDOWS))
     speeds = jnp.where(real, 0.45 * 1.1 ** (-(bins % NFREQ).astype(f32)), 0.0)
     angle = (bins // NFREQ).astype(f32) * (2.0 * jnp.pi / NDIR)
     abs_x = jnp.abs(speeds * jnp.cos(angle))
     abs_y = jnp.abs(speeds * jnp.sin(angle))
     stay = 1.0 - abs_x - abs_y
-    coef = jnp.broadcast_to(jnp.concatenate([abs_x / stay, abs_y / stay])[:, None], (2 * GROUP, LANES))
+    coef_x, coef_y = abs_x / stay, abs_y / stay
+    rest = [part for coef in (coef_x, coef_y) for part in 2 * [coef[GROUP : GROUP + HALF]]]
+    coef = jnp.concatenate([coef_x[:GROUP], coef_y[:GROUP], *rest])
+    coef = jnp.broadcast_to(coef[:, None], (4 * GROUP, LANES))
     scale = stay * stay * stay * stay
     up_x = (quad == 0) | (quad == 3)
     up_y = quad < 2
@@ -260,8 +311,7 @@
         table = table.reshape((NXG, COLS) + table.shape[1:])
         table = jnp.where(up_x, table, jnp.flip(table, 0))
         table = jnp.where(up_y, table, jnp.flip(table, 1))
-        table = table.reshape((BLOCKS,) + table.shape[2:])
-        return jnp.pad(table, ((DELAY * STEP, (ROUNDS - SLABS) * STEP),) + ((0, 0),) * (table.ndim - 1))
+        return table.reshape((BLOCKS,) + table.shape[2:])
 
     mask = land_mask.reshape(BLOCKS, LANES).astype(f32)
     upto = jnp.dot(mask, jnp.triu(jnp.ones((LANES, LANES), f32)), preferred_element_type=f32)
@@ -289,8 +339,9 @@
         out_shape=jax.ShapeDtypeStruct((ROWS, LANES), f32),
         in_specs=[pl.BlockSpec(memory_space=pltpu.SMEM)] * 5 + [pl.BlockSpec(memory_space=pltpu.VMEM)] * 5,
         out_specs=pl.BlockSpec(memory_space=pltpu.VMEM),
-        scratch_shapes=[pltpu.VMEM(((P_DEV + 2) * GROUP, LANES), f32)] * 2
-        + [pltpu.VMEM((SLAB * COLS * GROUP, LANES), f32)] * (2 * (SUB + 1)),
+        scratch_shapes=[pltpu.VMEM(((P_DEV + 2) * GROUP, LANES), f32)] * 4
+        + [pltpu.VMEM((SLAB * COLS * GROUP, LANES), f32)] * (2 * (SUB + 1))
+        + [pltpu.VMEM((SLAB * 2 * GROUP, LANES), f32)] * (2 * (SUB + 1)),
         compiler_params=pltpu.CompilerParams(vmem_limit_bytes=VMEM),
         name="propagate",
     )(*scalars, recv, *vectors)

time: 76.9 us -> 74 us (0.962)
  Pallas kernels: 15.3 us -> 12.4 us
    pallas_call x1, Pallas kernels: 11 us -> 8.12 us  [propagate(): pl.pallas_call(propagate_kernel, out_shape=jax.ShapeDtypeStruct((ROWS, LA...]
where the time goes in v4:
time: 74 us; the launch traced here: 73.8 us
  blocking collectives  26.9 us (36%)
  waiting for transfers between devices  18.8 us (25%)
  Pallas kernels  12.4 us (17%)
  starting transfers between devices  11.5 us (16%)
  local copies, waits for them, and re-layouts  2.11 us (3%)
  matrix products  1.09 us (1%)
    all_to_all x1, blocking collectives, exchange(): lax.all_to_all(rows.reshape(ROWS, 1, LANES), 'dev', split_axis=0, concat_...  26.9 us
    all_to_all x1, waiting for transfers between devices, exchange(): lax.all_to_all(rows.reshape(ROWS, 1, LANES), 'dev', split_axis=0, concat_...  18.8 us
    all_to_all x1, starting transfers between devices, exchange(): lax.all_to_all(rows.reshape(ROWS, 1, LANES), 'dev', split_axis=0, concat_...  11.5 us
    pallas_call x1, Pallas kernels, propagate(): pl.pallas_call(propagate_kernel, out_shape=jax.ShapeDtypeStruct((ROWS, LA...  8.12 us
    pallas_call x1, Pallas kernels, source_terms(): pl.pallas_call(source_kernel, out_shape=jax.ShapeDtypeStruct((ROWS, LANES...  3.18 us
  transfers between devices with their start and end apart: 1, of which 1 were waited for; matrix products, arithmetic and copies ran while one was open for 5% of the time, Pallas kernels for 0%

profile of v4, /device:TPU:1, one launch (start us, length us, event | category | flops | bytes accessed | tf_op | source)
XLA Modules:
  0.0 73.8 jit_solution(16752509613524431414)
XLA Ops:
  0.0 3.2 %source_terms.1 = f32[2688,128]{1,0:T(8,128)} custom-call(f32[1296,256]{1,0:T(8,128)} %bitcast.41, f32[1,256]{1,0:T(1,128)} %bitcast.48, f32[1,256]{1,0:T(1,128)} %bitcast.49, f32[36,36]{1,0:T(8,128)} %coupling_hbm.1), custom_call_target="tpu_custom_call" | custom-call | tf_op jit(solution)/shard_map/source_terms/pallas_call | solution.py:136
  3.2 0.0 copy-start
  3.2 11.5 %all-to-all-start = ((f32[2688,1,128]{2,1,0:T(1,128)}), f32[2688,1,128]{2,1,0:T(1,128)S(1)}, u32[]{:S(2)}, u32[]{:S(2)}) async-start(f32[2688,1,128]{2,1,0:T(1,128)} %bitcast.38), calls=%async_computation | async-start | bytes 2752512 | tf_op jit(solution)/shard_map/all_to_all | solution.py:381
  14.8 0.0 copy-done
  14.9 0.3 convolution_bitcast_fusion
  15.2 0.0 copy-start.1
  15.2 0.3 convolution_reduce_fusion
  15.5 0.1 copy.12
  15.6 0.1 convert_element_type.61
  15.7 0.1 convert_element_type.55
  15.8 0.1 convert_element_type.57
  16.0 0.1 rev.45
  16.0 0.1 rev.43
  16.2 0.1 reshape.77.line_ref
  16.3 0.1 reshape.78.off_ref
  16.4 0.1 rev.47
  16.5 0.1 reshape.79.end_ref
  16.6 0.0 copy-done.1
  16.7 0.1 copy.13
  16.9 0.2 fusion.2
  17.1 0.3 fusion
  17.4 0.1 reverse_select_fusion
  17.5 0.2 rev.49
  17.8 0.2 rev.51
  18.0 0.2 rev.53
  18.2 0.1 fusion.21
  18.3 0.1 slice.19
  18.4 0.1 slice.20
  18.5 0.1 concatenate.3
  18.6 0.1 pad_add_fusion.up_ref
  18.6 0.1 broadcast_select_fusion.1
  18.8 18.8 %all-to-all-done = f32[2688,1,128]{2,1,0:T(1,128)S(1)} async-done(((f32[2688,1,128]{2,1,0:T(1,128)}), f32[2688,1,128]{2,1,0:T(1,128)S(1)}, u32[]{:S(2)}, u32[]{:S(2)}) %all-to-all-start) | async-done | bytes 1376288 | tf_op jit(solution)/shard_map/all_to_all | solution.py:381
  37.6 0.1 broadcast_in_dim.40.coef_ref
  37.6 8.1 %propagate.1 = f32[2688,128]{1,0:T(8,128)S(1)} custom-call(s32[384]{0:T(512)S(1)} %reshape.77.line_ref, s32[384]{0:T(512)S(1)} %reshape.78.off_ref, s32[384]{0:T(512)S(1)} %reshape.79.end_ref, s32[2]{0:T(128)S(1)} %pad_add_fusion.up_ref, f32[16]{0:T(128)S(1)} %get-tuple-element.15.scale_ref, f32[2688,128]{1,0:T(8,128)S(1)} %bitcast.32, ...), custom_call_target="tpu_custom_call" | custom-call | tf_op jit(solution)/shard_map/propagate/pallas_call | solution.py:337
  45.7 26.9 %all_to_all.10 = f32[2688,1,128]{2,1,0:T(1,128)S(1)} all-to-all(f32[2688,1,128]{2,1,0:T(1,128)S(1)} %bitcast.33), channel_id=1, replica_groups=mesh['dev'=128] {'dev'}, dimensions={0} | all-to-all | bytes 2752512 | tf_op jit(solution)/shard_map/all_to_all | solution.py:381
  72.6 1.2 %collect.1 = f32[1296,256]{1,0:T(8,128)} custom-call(f32[2688,128]{1,0:T(8,128)S(1)} %bitcast.34), custom_call_target="tpu_custom_call" | custom-call | tf_op jit(solution)/shard_map/collect/pallas_call | solution.py:370
  (20 shorter events, 0.3 us)
Async XLA Ops:
  3.2 11.6 %copy-start = (s32[96,512]{1,0:T(8,128)S(1)}, s32[96,512]{1,0:T(8,128)}, u32[]{:S(2)}) copy-start(s32[96,512]{1,0:T(8,128)} %param.10) | copy-start | bytes 589828
  3.2 34.4 %all-to-all-start = ((f32[2688,1,128]{2,1,0:T(1,128)}), f32[2688,1,128]{2,1,0:T(1,128)S(1)}, u32[]{:S(2)}, u32[]{:S(2)}) async-start(f32[2688,1,128]{2,1,0:T(1,128)} %bitcast.38), calls=%async_computation | async-start | bytes 2752512 | tf_op jit(solution)/shard_map/all_to_all | solution.py:381
  15.2 1.5 %copy-start.1 = (s32[32768]{0:T(1024)S(1)}, s32[32768]{0:T(1024)}, u32[]{:S(2)}) copy-start(s32[32768]{0:T(1024)} %param.11) | copy-start | bytes 393220

commit v5 on v4

--- a/solution.py
+++ b/solution.py
@@ -31,10 +31,10 @@
 PAIR = 2 * NFREQ
 PARTS = 6
 PART = BINS // PARTS
-SLAB = 2
+SLAB = 4
 SLABS = NXG // SLAB
 STEP = SLAB * COLS
-UNROLL = 14
+UNROLL = 18
 ALONG_LANES = lax.GatherDimensionNumbers(
     offset_dims=(),
     collapsed_slice_dims=(1,),
@@ -154,7 +154,7 @@
 
 
 def propagate_kernel(
-    line_ref, off_ref, end_ref, up_ref, scale_ref, recv_ref, index_ref, mask_ref, spot_ref, coef_ref, out_ref, *scratch
+    line_ref, off_ref, up_ref, scale_ref, recv_ref, index_ref, mask_ref, spot_ref, turn_ref, coef_ref, out_ref, *scratch
 ):
     src, dst, src_rest, dst_rest, *bufs = scratch
     up_y = up_ref[0]
@@ -199,10 +199,9 @@
 
     def store(target, cell, taken):
         begin = line_ref[cell]
-        off = off_ref[cell]
-        end = end_ref[cell]
-        pltpu.store(target.at[lines(begin), :], taken, mask=(lane >= off) & (lane < end))
-        pltpu.store(target.at[lines(begin + GROUP), :], taken, mask=lane < end - LANES)
+        turn_of = wide(turn_ref, cell)
+        pltpu.store(target.at[lines(begin), :], taken, mask=turn_of == 1)
+        pltpu.store(target.at[lines(begin + GROUP), :], taken, mask=turn_of == 2)
 
     def scatter(cell, values):
         store(dst, cell, take(values, wide(spot_ref, cell)))
@@ -328,8 +327,11 @@
     two = jnp.dot((line[:, None] + 1 == lines).astype(f32), spot, preferred_element_type=f32)
     spots = jnp.where(jnp.arange(LANES) >= off[:, None], one, two).astype(jnp.int32)
 
-    scalars = [ordered(line * GROUP), ordered(off), ordered(end), jnp.stack([up_y.astype(jnp.int32), member % WINDOWS]), scale]
-    return scalars, [ordered(index), ordered(mask), ordered(spots), coef]
+    first = (jnp.arange(LANES) >= off[:, None]) & (jnp.arange(LANES) < end[:, None])
+    turns = jnp.where(first, 1, jnp.where(jnp.arange(LANES) < end[:, None] - LANES, 2, 0)).astype(jnp.int32)
+
+    scalars = [ordered(line * GROUP), ordered(off), jnp.stack([up_y.astype(jnp.int32), member % WINDOWS]), scale]
+    return scalars, [ordered(index), ordered(mask), ordered(spots), ordered(turns), coef]
 
 
 def propagate(recv, scalars, vectors):
@@ -337,7 +339,7 @@
     return pl.pallas_call(
         propagate_kernel,
         out_shape=jax.ShapeDtypeStruct((ROWS, LANES), f32),
-        in_specs=[pl.BlockSpec(memory_space=pltpu.SMEM)] * 5 + [pl.BlockSpec(memory_space=pltpu.VMEM)] * 5,
+        in_specs=[pl.BlockSpec(memory_space=pltpu.SMEM)] * 4 + [pl.BlockSpec(memory_space=pltpu.VMEM)] * 6,
         out_specs=pl.BlockSpec(memory_space=pltpu.VMEM),
         scratch_shapes=[pltpu.VMEM(((P_DEV + 2) * GROUP, LANES), f32)] * 4
         + [pltpu.VMEM((SLAB * COLS * GROUP, LANES), f32)] * (2 * (SUB + 1))

time: 74 us -> 73.5 us (level)
  waiting for transfers between devices: 18.8 us -> 18 us
    all_to_all x1, waiting for transfers between devices: 18.8 us -> 18 us  [exchange(): lax.all_to_all(rows.reshape(ROWS, 1, LANES), 'dev', split_axis=0, concat_...]
  transfers between devices with their start and end apart: 1 -> 1, of which waited for: 1 -> 1; matrix products, arithmetic and copies ran while one was open for 5% -> 6% of each run, Pallas kernels for 0% -> 0%
where the time goes in v5:
time: 73.5 us; the launch traced here: 73.3 us
  blocking collectives  26.9 us (37%)
  waiting for transfers between devices  18 us (24%)
  Pallas kernels  11.9 us (16%)
  starting transfers between devices  11.5 us (16%)
  local copies, waits for them, and re-layouts  2.36 us (3%)
  other arithmetic  1.11 us (2%)
  matrix products  1.09 us (1%)
    all_to_all x1, blocking collectives, exchange(): lax.all_to_all(rows.reshape(ROWS, 1, LANES), 'dev', split_axis=0, concat_...  26.9 us
    all_to_all x1, waiting for transfers between devices, exchange(): lax.all_to_all(rows.reshape(ROWS, 1, LANES), 'dev', split_axis=0, concat_...  18 us
    all_to_all x1, starting transfers between devices, exchange(): lax.all_to_all(rows.reshape(ROWS, 1, LANES), 'dev', split_axis=0, concat_...  11.5 us
    pallas_call x1, Pallas kernels, propagate(): pl.pallas_call(propagate_kernel, out_shape=jax.ShapeDtypeStruct((ROWS, LA...  7.57 us
    pallas_call x1, Pallas kernels, source_terms(): pl.pallas_call(source_kernel, out_shape=jax.ShapeDtypeStruct((ROWS, LANES...  3.18 us
  transfers between devices with their start and end apart: 1, of which 1 were waited for; matrix products, arithmetic and copies ran while one was open for 6% of the time, Pallas kernels for 0%

profile of v5, /device:TPU:1, one launch (start us, length us, event | category | flops | bytes accessed | tf_op | source)
XLA Modules:
  0.0 73.3 jit_solution(14340791784509654874)
XLA Ops:
  0.0 3.2 %source_terms.1 = f32[2688,128]{1,0:T(8,128)} custom-call(f32[1296,256]{1,0:T(8,128)} %bitcast.45, f32[1,256]{1,0:T(1,128)} %bitcast.51, f32[1,256]{1,0:T(1,128)} %bitcast.52, f32[36,36]{1,0:T(8,128)} %coupling_hbm.1), custom_call_target="tpu_custom_call" | custom-call | tf_op jit(solution)/shard_map/source_terms/pallas_call | solution.py:136
  3.2 0.0 copy-start
  3.2 11.5 %all-to-all-start = ((f32[2688,1,128]{2,1,0:T(1,128)}), f32[2688,1,128]{2,1,0:T(1,128)S(1)}, u32[]{:S(2)}, u32[]{:S(2)}) async-start(f32[2688,1,128]{2,1,0:T(1,128)} %bitcast.40), calls=%async_computation | async-start | bytes 2752512 | tf_op jit(solution)/shard_map/all_to_all | solution.py:383
  14.8 0.0 copy-done
  14.9 0.1 convert_element_type.58
  14.9 0.1 copy.12
  15.1 0.3 convolution_bitcast_fusion
  15.3 0.3 convolution_reduce_fusion
  15.7 0.1 ge.47
  15.8 0.1 convert_element_type.54
  16.0 0.1 rev.45
  16.0 0.1 rev.43
  16.2 0.1 reshape.102.line_ref
  16.3 0.0 copy-start.1
  16.3 0.1 reshape.103.off_ref
  16.5 0.1 copy.13
  16.6 0.2 rev.47
  16.9 0.2 rev.49
  17.1 0.1 lt.70
  17.3 0.1 lt.67
  17.4 0.0 copy-done.1
  17.4 0.2 fusion.2
  17.7 0.3 fusion
  17.9 0.5 select_select_fusion
  18.4 0.1 reverse_select_fusion
  18.5 0.2 rev.51
  18.8 0.2 rev.53
  19.0 0.1 fusion.22
  19.1 0.1 slice.19
  19.2 0.1 slice.20
  19.2 0.1 concatenate.3
  19.3 0.1 pad_add_fusion.up_ref
  19.4 0.1 broadcast_select_fusion.3
  19.4 0.1 broadcast_select_fusion.2
  19.6 18.0 %all-to-all-done = f32[2688,1,128]{2,1,0:T(1,128)S(1)} async-done(((f32[2688,1,128]{2,1,0:T(1,128)}), f32[2688,1,128]{2,1,0:T(1,128)S(1)}, u32[]{:S(2)}, u32[]{:S(2)}) %all-to-all-start) | async-done | bytes 1376288 | tf_op jit(solution)/shard_map/all_to_all | solution.py:383
  37.6 0.1 broadcast_in_dim.61.coef_ref
  37.6 7.6 %propagate.1 = f32[2688,128]{1,0:T(8,128)S(1)} custom-call(s32[384]{0:T(512)S(1)} %reshape.102.line_ref, s32[384]{0:T(512)S(1)} %reshape.103.off_ref, s32[2]{0:T(128)S(1)} %pad_add_fusion.up_ref, f32[16]{0:T(128)S(1)} %get-tuple-element.16.scale_ref, f32[2688,128]{1,0:T(8,128)S(1)} %bitcast.33, s32[384,128]{1,0:T(8,128)S(1)} %bitcast.36, ...), custom_call_target="tpu_custom_call" | custom-call | tf_op jit(solution)/shard_map/propagate/pallas_call | solution.py:339
  45.2 26.9 %all_to_all.10 = f32[2688,1,128]{2,1,0:T(1,128)S(1)} all-to-all(f32[2688,1,128]{2,1,0:T(1,128)S(1)} %bitcast.34), channel_id=1, replica_groups=mesh['dev'=128] {'dev'}, dimensions={0} | all-to-all | bytes 2752512 | tf_op jit(solution)/shard_map/all_to_all | solution.py:383
  72.1 1.2 %collect.1 = f32[1296,256]{1,0:T(8,128)} custom-call(f32[2688,128]{1,0:T(8,128)S(1)} %bitcast.35), custom_call_target="tpu_custom_call" | custom-call | tf_op jit(solution)/shard_map/collect/pallas_call | solution.py:372
  (18 shorter events, 0.3 us)
Async XLA Ops:
  3.2 11.6 %copy-start = (s32[96,512]{1,0:T(8,128)S(1)}, s32[96,512]{1,0:T(8,128)}, u32[]{:S(2)}) copy-start(s32[96,512]{1,0:T(8,128)} %param.10) | copy-start | bytes 589828
  3.2 34.4 %all-to-all-start = ((f32[2688,1,128]{2,1,0:T(1,128)}), f32[2688,1,128]{2,1,0:T(1,128)S(1)}, u32[]{:S(2)}, u32[]{:S(2)}) async-start(f32[2688,1,128]{2,1,0:T(1,128)} %bitcast.40), calls=%async_computation | async-start | bytes 2752512 | tf_op jit(solution)/shard_map/all_to_all | solution.py:383
  16.3 1.1 %copy-start.1 = (s32[32768]{0:T(1024)S(1)}, s32[32768]{0:T(1024)}, u32[]{:S(2)}) copy-start(s32[32768]{0:T(1024)} %param.11) | copy-start | bytes 393220

commit v6 on v5

--- a/solution.py
+++ b/solution.py
@@ -154,19 +154,19 @@
 
 
 def propagate_kernel(
-    line_ref, off_ref, up_ref, scale_ref, recv_ref, index_ref, mask_ref, spot_ref, turn_ref, coef_ref, out_ref, *scratch
+    meta_ref, recv_ref, index_ref, mask_ref, spot_ref, turn_ref, coef_ref, out_ref, *scratch
 ):
     src, dst, src_rest, dst_rest, *bufs = scratch
-    up_y = up_ref[0]
+    up_y = meta_ref[2 * BLOCKS]
     lane = lax.broadcasted_iota(jnp.int32, (GROUP, LANES), 1)
     low = lax.broadcasted_iota(jnp.int32, (GROUP, LANES), 0) < HALF
     edge = lane == jnp.where(up_y > 0, 0, LANES - 1)
     shift = jnp.where(up_y > 0, 1, LANES - 1)
 
     pieces = [(HALVES * slot + half, slot, half * LANES * GROUP) for slot in range(SLOTS) for half in range(HALVES)]
-    pieces.append((CHUNK - 1, SLOTS, up_ref[1] * (LANES // 2 * GROUP)))
+    pieces.append((CHUNK - 1, SLOTS, meta_ref[2 * BLOCKS + 1] * (LANES // 2 * GROUP)))
     for row, slot, begin in pieces:
-        part = recv_ref[pl.ds(row, N_DEV, stride=CHUNK), :].T * scale_ref[slot]
+        part = recv_ref[pl.ds(row, N_DEV, stride=CHUNK), :].T * coef_ref[4 * GROUP + slot : 4 * GROUP + slot + 1, :]
         if slot < GROUP:
             src[pl.ds(begin + slot, LANES, stride=GROUP), :] = part
         else:
@@ -198,7 +198,7 @@
         return slice(begin, begin + GROUP)
 
     def store(target, cell, taken):
-        begin = line_ref[cell]
+        begin = meta_ref[cell]
         turn_of = wide(turn_ref, cell)
         pltpu.store(target.at[lines(begin), :], taken, mask=turn_of == 1)
         pltpu.store(target.at[lines(begin + GROUP), :], taken, mask=turn_of == 2)
@@ -212,15 +212,15 @@
         store(dst_rest, cell + 2, pltpu.roll(taken, HALF, 0))
 
     def gather(cell):
-        begin = line_ref[cell]
-        both = jnp.where(lane >= off_ref[cell], src[lines(begin), :], src[lines(begin + GROUP), :])
+        begin = meta_ref[cell]
+        both = jnp.where(lane >= meta_ref[BLOCKS + cell], src[lines(begin), :], src[lines(begin + GROUP), :])
         return jnp.where(wide(mask_ref, cell) > 0, take(both, wide(index_ref, cell)), 0.0)
 
     def gather_rest(cell):
-        begin, other = line_ref[cell], line_ref[cell + 2]
+        begin, other = meta_ref[cell], meta_ref[cell + 2]
         one = jnp.where(low, src_rest[lines(begin), :], src_rest[lines(other), :])
         next_one = jnp.where(low, src_rest[lines(begin + GROUP), :], src_rest[lines(other + GROUP), :])
-        both = jnp.where(lane >= jnp.where(low, off_ref[cell], off_ref[cell + 2]), one, next_one)
+        both = jnp.where(lane >= jnp.where(low, meta_ref[BLOCKS + cell], meta_ref[BLOCKS + cell + 2]), one, next_one)
         return jnp.where(two(mask_ref, cell) > 0, take(both, two(index_ref, cell)), 0.0)
 
     def turn(fields):
@@ -298,11 +298,11 @@
     abs_x = jnp.abs(speeds * jnp.cos(angle))
     abs_y = jnp.abs(speeds * jnp.sin(angle))
     stay = 1.0 - abs_x - abs_y
+    scale = stay * stay * stay * stay
     coef_x, coef_y = abs_x / stay, abs_y / stay
     rest = [part for coef in (coef_x, coef_y) for part in 2 * [coef[GROUP : GROUP + HALF]]]
-    coef = jnp.concatenate([coef_x[:GROUP], coef_y[:GROUP], *rest])
-    coef = jnp.broadcast_to(coef[:, None], (4 * GROUP, LANES))
-    scale = stay * stay * stay * stay
+    coef = jnp.concatenate([coef_x[:GROUP], coef_y[:GROUP], *rest, scale])
+    coef = jnp.broadcast_to(coef[:, None], (4 * GROUP + HELD, LANES))
     up_x = (quad == 0) | (quad == 3)
     up_y = quad < 2
 
@@ -330,23 +330,24 @@
     first = (jnp.arange(LANES) >= off[:, None]) & (jnp.arange(LANES) < end[:, None])
     turns = jnp.where(first, 1, jnp.where(jnp.arange(LANES) < end[:, None] - LANES, 2, 0)).astype(jnp.int32)
 
-    scalars = [ordered(line * GROUP), ordered(off), jnp.stack([up_y.astype(jnp.int32), member % WINDOWS]), scale]
-    return scalars, [ordered(index), ordered(mask), ordered(spots), ordered(turns), coef]
-
-
-def propagate(recv, scalars, vectors):
+    signs = jnp.stack([up_y.astype(jnp.int32), member % WINDOWS])
+    meta = jnp.concatenate([ordered(line * GROUP), ordered(off), signs])
+    return meta, [ordered(index), ordered(mask), ordered(spots), ordered(turns), coef]
+
+
+def propagate(recv, meta, vectors):
     f32 = jnp.float32
     return pl.pallas_call(
         propagate_kernel,
         out_shape=jax.ShapeDtypeStruct((ROWS, LANES), f32),
-        in_specs=[pl.BlockSpec(memory_space=pltpu.SMEM)] * 4 + [pl.BlockSpec(memory_space=pltpu.VMEM)] * 6,
+        in_specs=[pl.BlockSpec(memory_space=pltpu.SMEM)] + [pl.BlockSpec(memory_space=pltpu.VMEM)] * 6,
         out_specs=pl.BlockSpec(memory_space=pltpu.VMEM),
         scratch_shapes=[pltpu.VMEM(((P_DEV + 2) * GROUP, LANES), f32)] * 4
         + [pltpu.VMEM((SLAB * COLS * GROUP, LANES), f32)] * (2 * (SUB + 1))
         + [pltpu.VMEM((SLAB * 2 * GROUP, LANES), f32)] * (2 * (SUB + 1)),
         compiler_params=pltpu.CompilerParams(vmem_limit_bytes=VMEM),
         name="propagate",
-    )(*scalars, recv, *vectors)
+    )(meta, recv, *vectors)
 
 
 def collect_kernel(in_ref, out_ref):

time: 73.5 us -> 73.5 us (level)
  no operation moved by 1% of the time
where the time goes in v6:
time: 73.5 us; the launch traced here: 73.3 us
  blocking collectives  26.9 us (37%)
  waiting for transfers between devices  17.9 us (24%)
  Pallas kernels  11.9 us (16%)
  starting transfers between devices  11.5 us (16%)
  local copies, waits for them, and re-layouts  2.36 us (3%)
  other arithmetic  1.17 us (2%)
  matrix products  1.09 us (1%)
    all_to_all x1, blocking collectives, exchange(): lax.all_to_all(rows.reshape(ROWS, 1, LANES), 'dev', split_axis=0, concat_...  26.9 us
    all_to_all x1, waiting for transfers between devices, exchange(): lax.all_to_all(rows.reshape(ROWS, 1, LANES), 'dev', split_axis=0, concat_...  17.9 us
    all_to_all x1, starting transfers between devices, exchange(): lax.all_to_all(rows.reshape(ROWS, 1, LANES), 'dev', split_axis=0, concat_...  11.5 us
    pallas_call x1, Pallas kernels, propagate(): pl.pallas_call(propagate_kernel, out_shape=jax.ShapeDtypeStruct((ROWS, LA...  7.61 us
    pallas_call x1, Pallas kernels, source_terms(): pl.pallas_call(source_kernel, out_shape=jax.ShapeDtypeStruct((ROWS, LANES...  3.18 us
  transfers between devices with their start and end apart: 1, of which 1 were waited for; matrix products, arithmetic and copies ran while one was open for 6% of the time, Pallas kernels for 0%

profile of v6, /device:TPU:1, one launch (start us, length us, event | category | flops | bytes accessed | tf_op | source)
XLA Modules:
  0.0 73.3 jit_solution(17104952686455207116)
XLA Ops:
  0.0 3.2 %source_terms.1 = f32[2688,128]{1,0:T(8,128)} custom-call(f32[1296,256]{1,0:T(8,128)} %bitcast.39, f32[1,256]{1,0:T(1,128)} %bitcast.42, f32[1,256]{1,0:T(1,128)} %bitcast.43, f32[36,36]{1,0:T(8,128)} %coupling_hbm.1), custom_call_target="tpu_custom_call" | custom-call | tf_op jit(solution)/shard_map/source_terms/pallas_call | solution.py:136
  3.2 0.0 copy-start
  3.2 11.5 %all-to-all-start = ((f32[2688,1,128]{2,1,0:T(1,128)}), f32[2688,1,128]{2,1,0:T(1,128)S(1)}, u32[]{:S(2)}, u32[]{:S(2)}) async-start(f32[2688,1,128]{2,1,0:T(1,128)} %bitcast.34), calls=%async_computation | async-start | bytes 2752512 | tf_op jit(solution)/shard_map/all_to_all | solution.py:384
  14.8 0.0 copy-done
  14.8 0.1 convert_element_type.56
  14.9 0.1 copy.12
  15.0 0.3 convolution_bitcast_fusion
  15.3 0.3 convolution_reduce_fusion
  15.7 0.1 ge.47
  15.8 0.1 convert_element_type.54
  16.0 0.1 rev.45
  16.1 0.1 rev.43
  16.2 0.1 reshape.103
  16.3 0.1 reshape.102
  16.4 0.1 copy.13
  16.6 0.0 copy-start.1
  16.6 0.2 rev.47
  16.9 0.2 rev.49
  17.1 0.1 lt.66
  17.2 0.1 lt.63
  17.3 0.5 select_select_fusion
  17.9 0.2 rev.53
  18.1 0.0 copy-done.1
  18.2 0.2 fusion.2
  18.4 0.3 fusion
  18.7 0.2 rev.51
  19.0 0.1 multiply_multiply_fusion
  19.1 0.1 slice.19
  19.2 0.1 slice.20
  19.2 0.1 concatenate.7
  19.3 0.1 pad_add_fusion.meta_ref
  19.4 0.1 broadcast_select_fusion.3
  19.5 0.1 broadcast_select_fusion.2
  19.5 0.1 broadcast_select_fusion
  19.7 17.9 %all-to-all-done = f32[2688,1,128]{2,1,0:T(1,128)S(1)} async-done(((f32[2688,1,128]{2,1,0:T(1,128)}), f32[2688,1,128]{2,1,0:T(1,128)S(1)}, u32[]{:S(2)}, u32[]{:S(2)}) %all-to-all-start) | async-done | bytes 1376288 | tf_op jit(solution)/shard_map/all_to_all | solution.py:384
  37.6 0.1 broadcast_in_dim.61.coef_ref
  37.6 7.6 %propagate.1 = f32[2688,128]{1,0:T(8,128)S(1)} custom-call(s32[770]{0:T(1024)S(1)} %pad_add_fusion.meta_ref, f32[2688,128]{1,0:T(8,128)S(1)} %bitcast.27, s32[384,128]{1,0:T(8,128)S(1)} %bitcast.30, f32[384,128]{1,0:T(8,128)S(1)} %bitcast.31, s32[384,128]{1,0:T(8,128)S(1)} %bitcast.33, s32[384,128]{1,0:T(8,128)S(1)} %bitcast.32, ...), custom_call_target="tpu_custom_call" | custom-call | tf_op jit(solution)/shard_map/propagate/pallas_call | solution.py:340
  45.2 26.9 %all_to_all.10 = f32[2688,1,128]{2,1,0:T(1,128)S(1)} all-to-all(f32[2688,1,128]{2,1,0:T(1,128)S(1)} %bitcast.28), channel_id=1, replica_groups=mesh['dev'=128] {'dev'}, dimensions={0} | all-to-all | bytes 2752512 | tf_op jit(solution)/shard_map/all_to_all | solution.py:384
  72.1 1.2 %collect.1 = f32[1296,256]{1,0:T(8,128)} custom-call(f32[2688,128]{1,0:T(8,128)S(1)} %bitcast.29), custom_call_target="tpu_custom_call" | custom-call | tf_op jit(solution)/shard_map/collect/pallas_call | solution.py:373
  (18 shorter events, 0.4 us)
Async XLA Ops:
  3.2 11.6 %copy-start = (s32[96,512]{1,0:T(8,128)S(1)}, s32[96,512]{1,0:T(8,128)}, u32[]{:S(2)}) copy-start(s32[96,512]{1,0:T(8,128)} %param.10) | copy-start | bytes 589828
  3.2 34.4 %all-to-all-start = ((f32[2688,1,128]{2,1,0:T(1,128)}), f32[2688,1,128]{2,1,0:T(1,128)S(1)}, u32[]{:S(2)}, u32[]{:S(2)}) async-start(f32[2688,1,128]{2,1,0:T(1,128)} %bitcast.34), calls=%async_computation | async-start | bytes 2752512 | tf_op jit(solution)/shard_map/all_to_all | solution.py:384
  16.6 1.6 %copy-start.1 = (s32[32768]{0:T(1024)S(1)}, s32[32768]{0:T(1024)}, u32[]{:S(2)}) copy-start(s32[32768]{0:T(1024)} %param.11) | copy-start | bytes 393220
